TPU v7x, 32 devices: a whole 2x2x4 slice. The times are simulated.
32 devices in a mesh: gx: 8 (over z, x), gy: 4 (over y, core).
Axes of the slice: x: 2, y: 2, z: 4, core: 2. Of those that a mesh axis runs over, the one named last changes fastest.
Arguments:
- patches: bfloat16 [13824, 768], P(('gx', 'gy')), may hold values from -6 to 6
- clip_of_row: int32 [13824], P('gx'), may hold values from 0 to 15, as said below
- position_of_row: int32 [13824], P(('gx', 'gy')), may hold values from 0 to 1213, as said below
- pos_embed: bfloat16 [1214, 768], P(None, ('gx', 'gy')), may hold values from -3 to 3
- norm1_gain: bfloat16 [2, 768], P(None, ('gx', 'gy')), may hold values from 0.5 to 1.5
- norm1_bias: bfloat16 [2, 768], P(None, ('gx', 'gy')), may hold values from -1.5 to 1.5
- query_bias: bfloat16 [2, 768], P(None, ('gx', 'gy')), may hold values from -1.5 to 1.5
- value_bias: bfloat16 [2, 768], P(None, ('gx', 'gy')), may hold values from -1.5 to 1.5
- out_bias: bfloat16 [2, 768], P(None, ('gx', 'gy')), may hold values from -1.5 to 1.5
- norm2_gain: bfloat16 [2, 768], P(None, ('gx', 'gy')), may hold values from 0.5 to 1.5
- norm2_bias: bfloat16 [2, 768], P(None, ('gx', 'gy')), may hold values from -1.5 to 1.5
- up_bias: bfloat16 [2, 3072], P(None, ('gx', 'gy')), may hold values from -1.5 to 1.5
- down_bias: bfloat16 [2, 768], P(None, ('gx', 'gy')), may hold values from -1.5 to 1.5
- qkv_weight: bfloat16 [2, 768, 2304], P(None, ('gx', 'gy')), may hold values from -0.21875 to 0.21875
- out_weight: bfloat16 [2, 768, 768], P(None, ('gx', 'gy')), may hold values from -4 to 4
- up_weight: bfloat16 [2, 768, 3072], P(None, 'gx', 'gy'), may hold values from -0.21875 to 0.21875
- down_weight: bfloat16 [2, 3072, 768], P(None, 'gy', 'gx'), may hold values from -0.109375 to 0.109375
- cotangent: bfloat16 [13824, 768], P(('gx', 'gy')), may hold values from -6 to 6
Outputs:
- activations: float32 [13824, 768], P(('gx', 'gy'))
- input_grad: float32 [13824, 768], P(('gx', 'gy'))
- pos_embed_grad: float32 [1214, 768], P(None, ('gx', 'gy'))
- norm1_gain_grad: float32 [2, 768], P(None, ('gx', 'gy'))
- norm1_bias_grad: float32 [2, 768], P(None, ('gx', 'gy'))
- query_bias_grad: float32 [2, 768], P(None, ('gx', 'gy'))
- value_bias_grad: float32 [2, 768], P(None, ('gx', 'gy'))
- out_bias_grad: float32 [2, 768], P(None, ('gx', 'gy'))
- norm2_gain_grad: float32 [2, 768], P(None, ('gx', 'gy'))
- norm2_bias_grad: float32 [2, 768], P(None, ('gx', 'gy'))
- up_bias_grad: float32 [2, 3072], P(None, ('gx', 'gy'))
- down_bias_grad: float32 [2, 768], P(None, ('gx', 'gy'))
- qkv_weight_grad: float32 [2, 768, 2304], P(None, ('gx', 'gy'))
- out_weight_grad: float32 [2, 768, 768], P(None, ('gx', 'gy'))
- up_weight_grad: float32 [2, 768, 3072], P(None, 'gx', 'gy')
- down_weight_grad: float32 [2, 3072, 768], P(None, 'gy', 'gx')
Inputs may be any that keep to these rules, and one draw needn't show every extreme that they name: `clip_of_row`: rows of one clip lie within one aligned block of 1728 rows; each block holds 1 clips of 1214 rows and 1 clips of 514 rows, and each clip number names one clip. Each of the block's 432-row pieces holds the length of every clip of the block divided by 4, rounded down or up, of its rows. `position_of_row`: A clip of 1214 rows uses each position 0 to 1213 once. A clip of 514 rows uses 0 and 1 for its two class tokens and, by a one-dimensional nearest-index map over the flattened table (not a two-dimensional interpolation of the frequency and time grid), 2 + ((k - 2) * 1212) // 512 for its other tokens k = 2 to 513.
All inputs are finite; a program needn't handle non-finite values.
Results may differ from a plain program's by a relative error of at most 0.014.
Values may be sent and summed in bfloat16 or wider, within the bound.
A program may use at most 192 MiB of HBM per device.

v0:
```python
import math

import jax
import jax.numpy as jnp
from jax import lax
from jax.sharding import PartitionSpec as P

HEAD_DIM = 64


EPSILON = 1e-06
SQRT_HALF = 1.0 / math.sqrt(2.0)
NORMAL_PEAK = 1.0 / math.sqrt(2.0 * math.pi)
MASKED = -1e30


def layer_norm(values, norm_gain, norm_shift):
    row_mean = jnp.mean(values, axis=-1, keepdims=True)
    centred = values - row_mean
    row_var = jnp.mean(centred * centred, axis=-1, keepdims=True)
    return centred * lax.rsqrt(row_var + EPSILON) * norm_gain + norm_shift


def gelu_slope(pre_act):
    return (
        0.5 * (1.0 + lax.erf(pre_act * SQRT_HALF))
        + pre_act * jnp.exp(-0.5 * pre_act * pre_act) * NORMAL_PEAK
    )


def column_pair(matrix, pair_index, pair_width):
    block = lax.dynamic_slice_in_dim(matrix, pair_index * pair_width, pair_width, 1)
    return block.reshape(matrix.shape[0], 2, pair_width // 2)


def join_pairs(stacked):
    return jnp.transpose(stacked, (1, 0, 2)).reshape(
        stacked.shape[1], stacked.shape[0] * stacked.shape[2]
    )


def pair_scores(head_query, head_keys, same_clip):
    scores = jnp.einsum(
        "qhd,khd->hqk", head_query, head_keys, preferred_element_type=jnp.float32
    ) * HEAD_DIM ** (-0.5)
    return jnp.where(same_clip[None], scores, MASKED)


def pair_parts(head_query, head_keys, head_values, head_grad, same_clip, pair_total):
    scores = pair_scores(head_query, head_keys, same_clip)
    weights = jnp.exp(scores - pair_total)
    weight_grad = jnp.einsum(
        "qhd,khd->hqk", head_grad, head_values, preferred_element_type=jnp.float32
    )
    return (weights, weight_grad)


def attend(queries, key_rows, value_rows, same_clip):
    pair_width = 2 * HEAD_DIM
    pair_count = queries.shape[1] // pair_width

    def one_pair(pair_index):
        head_query = column_pair(queries, pair_index, pair_width)
        head_keys = column_pair(key_rows, pair_index, pair_width)
        head_values = column_pair(value_rows, pair_index, pair_width)
        scores = pair_scores(head_query, head_keys, same_clip)
        row_max = jnp.max(scores, axis=-1, keepdims=True)
        log_total = row_max + jnp.log(jnp.sum(jnp.exp(scores - row_max), axis=-1, keepdims=True))
        weights = jnp.exp(scores - log_total).astype(jnp.bfloat16)
        mixed = jnp.einsum("hqk,khd->qhd", weights, head_values, preferred_element_type=jnp.float32)
        return (mixed.reshape(queries.shape[0], pair_width), log_total)

    mixed, log_total = lax.map(one_pair, jnp.arange(pair_count))
    return (join_pairs(mixed), log_total)


def attend_back(queries, key_rows, value_rows, same_clip, log_total, mixed_grad):
    pair_width = 2 * HEAD_DIM
    pair_count = queries.shape[1] // pair_width
    score_scale = HEAD_DIM ** (-0.5)

    def one_pair(pair_inputs):
        pair_index, pair_total = pair_inputs
        head_query = column_pair(queries, pair_index, pair_width)
        head_keys = column_pair(key_rows, pair_index, pair_width)
        head_values = column_pair(value_rows, pair_index, pair_width)
        head_grad = column_pair(mixed_grad, pair_index, pair_width)
        weights, weight_grad = pair_parts(
            head_query, head_keys, head_values, head_grad, same_clip, pair_total
        )
        value_grad = jnp.einsum(
            "hqk,qhd->khd",
            weights.astype(jnp.bfloat16),
            head_grad,
            preferred_element_type=jnp.float32,
        )
        inner = jnp.sum(weights * weight_grad, axis=-1, keepdims=True)
        score_grad = (weights * (weight_grad - inner)).astype(jnp.bfloat16)
        query_grad = (
            jnp.einsum("hqk,khd->qhd", score_grad, head_keys, preferred_element_type=jnp.float32)
            * score_scale
        )
        key_grad = (
            jnp.einsum("hqk,qhd->khd", score_grad, head_query, preferred_element_type=jnp.float32)
            * score_scale
        )
        return (
            query_grad.reshape(queries.shape[0], pair_width),
            key_grad.reshape(key_rows.shape[0], pair_width),
            value_grad.reshape(key_rows.shape[0], pair_width),
        )

    query_grad, key_grad, value_grad = lax.map(one_pair, (jnp.arange(pair_count), log_total))
    return (join_pairs(query_grad), join_pairs(key_grad), join_pairs(value_grad))


def stacked_member(collected, member_index):
    return jnp.stack([entry[member_index] for entry in collected])


def shards(
    patches,
    clip_of_row,
    position_of_row,
    pos_embed,
    norm1_gain,
    norm1_bias,
    query_bias,
    value_bias,
    out_bias,
    norm2_gain,
    norm2_bias,
    up_bias,
    down_bias,
    qkv_weight,
    out_weight,
    up_weight,
    down_weight,
    cotangent,
):
    (
        position_table,
        gain_one,
        shift_one,
        bias_query,
        bias_value,
        bias_out,
        gain_two,
        shift_two,
        bias_up,
        bias_down,
        weight_qkv,
        weight_out,
    ) = (
        lax.all_gather(pos_embed, ("gx", "gy"), axis=1, tiled=True),
        lax.all_gather(norm1_gain, ("gx", "gy"), axis=1, tiled=True),
        lax.all_gather(norm1_bias, ("gx", "gy"), axis=1, tiled=True),
        lax.all_gather(query_bias, ("gx", "gy"), axis=1, tiled=True),
        lax.all_gather(value_bias, ("gx", "gy"), axis=1, tiled=True),
        lax.all_gather(out_bias, ("gx", "gy"), axis=1, tiled=True),
        lax.all_gather(norm2_gain, ("gx", "gy"), axis=1, tiled=True),
        lax.all_gather(norm2_bias, ("gx", "gy"), axis=1, tiled=True),
        lax.all_gather(up_bias, ("gx", "gy"), axis=1, tiled=True),
        lax.all_gather(down_bias, ("gx", "gy"), axis=1, tiled=True),
        lax.all_gather(qkv_weight, ("gx", "gy"), axis=1, tiled=True),
        lax.all_gather(out_weight, ("gx", "gy"), axis=1, tiled=True),
    )
    block_up, block_down = (
        lax.all_gather(up_weight, "gx", axis=1, tiled=True),
        lax.all_gather(down_weight, "gx", axis=2, tiled=True),
    )
    layer_count = qkv_weight.shape[0]
    features = patches.shape[1]
    row_count = patches.shape[0]
    hidden_width = block_up.shape[2]
    member = lax.axis_index("gy")
    hidden_start = member * hidden_width
    own_clip = lax.dynamic_slice_in_dim(clip_of_row, member * row_count, row_count)
    same_clip = own_clip[:, None] == clip_of_row[None, :]
    state = patches.astype(jnp.float32) + position_table[position_of_row].astype(jnp.float32)
    stored = []
    for layer_index in range(layer_count):
        norm_gain_one = gain_one[layer_index].astype(jnp.float32)
        norm_shift_one = shift_one[layer_index].astype(jnp.float32)
        act_one = layer_norm(state, norm_gain_one, norm_shift_one).astype(jnp.bfloat16)
        projected = jnp.dot(act_one, weight_qkv[layer_index], preferred_element_type=jnp.float32)
        queries = (projected[:, :features] + bias_query[layer_index].astype(jnp.float32)).astype(
            jnp.bfloat16
        )
        key_rows = projected[:, features : 2 * features].astype(jnp.bfloat16)
        value_rows = (
            projected[:, 2 * features :] + bias_value[layer_index].astype(jnp.float32)
        ).astype(jnp.bfloat16)
        all_keys, all_values = (
            lax.all_gather(key_rows, "gy", axis=0, tiled=True),
            lax.all_gather(value_rows, "gy", axis=0, tiled=True),
        )
        mixed, log_total = attend(queries, all_keys, all_values, same_clip)
        attended = mixed.astype(jnp.bfloat16)
        middle = (
            state
            + jnp.dot(attended, weight_out[layer_index], preferred_element_type=jnp.float32)
            + bias_out[layer_index].astype(jnp.float32)
        )
        norm_gain_two = gain_two[layer_index].astype(jnp.float32)
        norm_shift_two = shift_two[layer_index].astype(jnp.float32)
        act_two = layer_norm(middle, norm_gain_two, norm_shift_two).astype(jnp.bfloat16)
        up_columns = lax.dynamic_slice_in_dim(
            bias_up[layer_index], hidden_start, hidden_width
        ).astype(jnp.float32)
        mlp_rows = lax.all_gather(act_two, "gy", axis=0, tiled=True)
        pre_act = (
            jnp.dot(mlp_rows, block_up[layer_index], preferred_element_type=jnp.float32)
            + up_columns
        )
        hidden = jax.nn.gelu(pre_act, approximate=False).astype(jnp.bfloat16)
        partial_out = jnp.dot(hidden, block_down[layer_index], preferred_element_type=jnp.float32)
        mlp_out = lax.psum_scatter(
            partial_out.astype(jnp.bfloat16), "gy", scatter_dimension=0, tiled=True
        ).astype(jnp.float32)
        stored.append(
            (
                state,
                act_one,
                queries,
                key_rows,
                value_rows,
                all_keys,
                all_values,
                log_total,
                attended,
                middle,
                mlp_rows,
                pre_act,
                hidden,
            )
        )
        state = middle + mlp_out + bias_down[layer_index].astype(jnp.float32)
    gradient = cotangent.astype(jnp.float32)
    collected = [None] * layer_count
    for layer_index in reversed(range(layer_count)):
        (
            layer_input,
            act_one,
            queries,
            key_rows,
            value_rows,
            kept_keys,
            kept_values,
            log_total,
            attended,
            middle,
            mlp_rows,
            pre_act,
            hidden,
        ) = stored[layer_index]
        grad_two = gradient.astype(jnp.bfloat16)
        down_bias_part = jnp.sum(grad_two.astype(jnp.float32), axis=0)
        grad_rows = lax.all_gather(grad_two, "gy", axis=0, tiled=True)
        down_part = jnp.einsum("rf,rd->fd", hidden, grad_rows, preferred_element_type=jnp.float32)
        hidden_grad = jnp.einsum(
            "rd,fd->rf", grad_rows, block_down[layer_index], preferred_element_type=jnp.float32
        )
        pre_grad = (hidden_grad * gelu_slope(pre_act)).astype(jnp.bfloat16)
        up_part = jnp.einsum("rd,rf->df", mlp_rows, pre_grad, preferred_element_type=jnp.float32)
        up_columns_grad = jnp.sum(pre_grad.astype(jnp.float32), axis=0)
        up_bias_part = lax.dynamic_update_slice_in_dim(
            jnp.zeros((bias_up.shape[1],), jnp.float32), up_columns_grad, hidden_start, 0
        )
        rows_grad = jnp.einsum(
            "rf,df->rd", pre_grad, block_up[layer_index], preferred_element_type=jnp.float32
        )
        act_two_grad = lax.psum_scatter(
            rows_grad.astype(jnp.bfloat16), "gy", scatter_dimension=0, tiled=True
        ).astype(jnp.float32)
        norm_gain_two = gain_two[layer_index].astype(jnp.float32)
        norm_shift_two = shift_two[layer_index].astype(jnp.float32)
        unused_two, norm_two_pull = jax.vjp(layer_norm, middle, norm_gain_two, norm_shift_two)
        middle_part, gain_two_part, shift_two_part = norm_two_pull(act_two_grad)
        mid_grad = gradient + middle_part
        grad_one = mid_grad.astype(jnp.bfloat16)
        out_bias_part = jnp.sum(grad_one.astype(jnp.float32), axis=0)
        out_part = jnp.einsum("rd,re->de", attended, grad_one, preferred_element_type=jnp.float32)
        mixed_grad = jnp.einsum(
            "re,de->rd", grad_one, weight_out[layer_index], preferred_element_type=jnp.float32
        ).astype(jnp.bfloat16)
        query_grad, key_grad, value_grad = attend_back(
            queries, kept_keys, kept_values, same_clip, log_total, mixed_grad
        )
        key_grad, value_grad = (
            lax.psum_scatter(
                key_grad.astype(jnp.bfloat16), "gy", scatter_dimension=0, tiled=True
            ).astype(jnp.float32),
            lax.psum_scatter(
                value_grad.astype(jnp.bfloat16), "gy", scatter_dimension=0, tiled=True
            ).astype(jnp.float32),
        )
        qkv_grad = jnp.concatenate(
            [
                query_grad.astype(jnp.bfloat16),
                key_grad.astype(jnp.bfloat16),
                value_grad.astype(jnp.bfloat16),
            ],
            axis=1,
        )
        query_bias_part = jnp.sum(qkv_grad[:, :features].astype(jnp.float32), axis=0)
        value_bias_part = jnp.sum(qkv_grad[:, 2 * features :].astype(jnp.float32), axis=0)
        qkv_part = jnp.einsum("rd,re->de", act_one, qkv_grad, preferred_element_type=jnp.float32)
        act_one_grad = jnp.einsum(
            "re,de->rd", qkv_grad, weight_qkv[layer_index], preferred_element_type=jnp.float32
        )
        norm_gain_one = gain_one[layer_index].astype(jnp.float32)
        norm_shift_one = shift_one[layer_index].astype(jnp.float32)
        unused_one, norm_one_pull = jax.vjp(layer_norm, layer_input, norm_gain_one, norm_shift_one)
        input_part, gain_one_part, shift_one_part = norm_one_pull(act_one_grad)
        gradient = mid_grad + input_part
        collected[layer_index] = (
            gain_one_part,
            shift_one_part,
            query_bias_part,
            value_bias_part,
            out_bias_part,
            gain_two_part,
            shift_two_part,
            up_bias_part,
            down_bias_part,
            qkv_part,
            out_part,
            up_part,
            down_part,
        )
    table_part = jax.ops.segment_sum(
        gradient, position_of_row, num_segments=position_table.shape[0]
    )
    (
        pos_embed_grad,
        norm1_gain_grad,
        norm1_bias_grad,
        query_bias_grad,
        value_bias_grad,
        out_bias_grad,
        norm2_gain_grad,
        norm2_bias_grad,
        up_bias_grad,
        down_bias_grad,
        qkv_weight_grad,
        out_weight_grad,
    ) = (
        lax.psum_scatter(table_part, ("gx", "gy"), scatter_dimension=1, tiled=True),
        lax.psum_scatter(
            stacked_member(collected, 0), ("gx", "gy"), scatter_dimension=1, tiled=True
        ),
        lax.psum_scatter(
            stacked_member(collected, 1), ("gx", "gy"), scatter_dimension=1, tiled=True
        ),
        lax.psum_scatter(
            stacked_member(collected, 2), ("gx", "gy"), scatter_dimension=1, tiled=True
        ),
        lax.psum_scatter(
            stacked_member(collected, 3), ("gx", "gy"), scatter_dimension=1, tiled=True
        ),
        lax.psum_scatter(
            stacked_member(collected, 4), ("gx", "gy"), scatter_dimension=1, tiled=True
        ),
        lax.psum_scatter(
            stacked_member(collected, 5), ("gx", "gy"), scatter_dimension=1, tiled=True
        ),
        lax.psum_scatter(
            stacked_member(collected, 6), ("gx", "gy"), scatter_dimension=1, tiled=True
        ),
        lax.psum_scatter(
            stacked_member(collected, 7), ("gx", "gy"), scatter_dimension=1, tiled=True
        ),
        lax.psum_scatter(
            stacked_member(collected, 8), ("gx", "gy"), scatter_dimension=1, tiled=True
        ),
        lax.psum_scatter(
            stacked_member(collected, 9), ("gx", "gy"), scatter_dimension=1, tiled=True
        ),
        lax.psum_scatter(
            stacked_member(collected, 10), ("gx", "gy"), scatter_dimension=1, tiled=True
        ),
    )
    up_stack = stacked_member(collected, 11)
    down_stack = stacked_member(collected, 12)
    up_weight_grad, down_weight_grad = (
        lax.psum_scatter(
            up_stack.astype(jnp.bfloat16), "gx", scatter_dimension=1, tiled=True
        ).astype(jnp.float32),
        lax.psum_scatter(
            down_stack.astype(jnp.bfloat16), "gx", scatter_dimension=2, tiled=True
        ).astype(jnp.float32),
    )
    return (
        state,
        gradient,
        pos_embed_grad,
        norm1_gain_grad,
        norm1_bias_grad,
        query_bias_grad,
        value_bias_grad,
        out_bias_grad,
        norm2_gain_grad,
        norm2_bias_grad,
        up_bias_grad,
        down_bias_grad,
        qkv_weight_grad,
        out_weight_grad,
        up_weight_grad,
        down_weight_grad,
    )


def solution(mesh):
    return jax.shard_map(
        shards,
        mesh=mesh,
        in_specs=(
            P(("gx", "gy"), None),
            P("gx"),
            P(("gx", "gy")),
            P(None, ("gx", "gy")),
            P(None, ("gx", "gy")),
            P(None, ("gx", "gy")),
            P(None, ("gx", "gy")),
            P(None, ("gx", "gy")),
            P(None, ("gx", "gy")),
            P(None, ("gx", "gy")),
            P(None, ("gx", "gy")),
            P(None, ("gx", "gy")),
            P(None, ("gx", "gy")),
            P(None, ("gx", "gy"), None),
            P(None, ("gx", "gy"), None),
            P(None, "gx", "gy"),
            P(None, "gy", "gx"),
            P(("gx", "gy"), None),
        ),
        out_specs=(
            P(("gx", "gy"), None),
            P(("gx", "gy"), None),
            P(None, ("gx", "gy")),
            P(None, ("gx", "gy")),
            P(None, ("gx", "gy")),
            P(None, ("gx", "gy")),
            P(None, ("gx", "gy")),
            P(None, ("gx", "gy")),
            P(None, ("gx", "gy")),
            P(None, ("gx", "gy")),
            P(None, ("gx", "gy")),
            P(None, ("gx", "gy")),
            P(None, ("gx", "gy"), None),
            P(None, ("gx", "gy"), None),
            P(None, "gx", "gy"),
            P(None, "gy", "gx"),
        ),
        check_vma=False,
    )
```

profile of v0, /device:TPU:0, one launch (start us, length us, event | category | flops | bytes accessed | tf_op | source)
XLA Modules:
  0.0 1889.1 jit_solution(5792434607289894951)
XLA Ops:
  8.7 43.2 %all-gather = bf16[32,24,2]{1,2,0:T(2,128)(2,1)S(1)} all-gather(bf16[1,24,2]{1,2,0:T(2,128)(2,1)} %bitcast.439), channel_id=1, replica_groups=mesh['gx'=8,'gy'=4] {'gx','gy'}, dimensions={0}, use_global_device_ids=true | all-gather | bytes 3168 | tf_op jit(solution)/shard_map/all_gather | solution.py:156
  52.0 36.6 %all-gather.1 = bf16[32,24,2]{1,2,0:T(2,128)(2,1)S(1)} all-gather(bf16[1,24,2]{1,2,0:T(2,128)(2,1)} %bitcast.440), channel_id=1, replica_groups=mesh['gx'=8,'gy'=4] {'gx','gy'}, dimensions={0}, use_global_device_ids=true | all-gather | bytes 3168 | tf_op jit(solution)/shard_map/all_gather | solution.py:157
  95.0 49.2 %all-gather.25.cloned.1.call-done = bf16[2,768,2304]{2,1,0:T(8,128)(2,1)} async-done(((bf16[2,24,2304]{2,1,0:T(8,128)(2,1)}), bf16[2,768,2304]{2,1,0:T(8,128)(2,1)}) %all-gather.25.cloned.1.call-update) | async-done | bytes 7077904 | tf_op jit(solution)/shard_map/all_gather | solution.py:165
  151.2 38.9 %all-gather.3 = bf16[32,24,2]{1,2,0:T(2,128)(2,1)S(1)} all-gather(bf16[1,24,2]{1,2,0:T(2,128)(2,1)S(1)} %bitcast.441), channel_id=1, replica_groups=mesh['gx'=8,'gy'=4] {'gx','gy'}, dimensions={0}, use_global_device_ids=true | all-gather | bytes 3168 | tf_op jit(solution)/shard_map/all_gather | solution.py:158
  190.2 36.4 %all-gather.2 = bf16[32,24,2]{1,2,0:T(2,128)(2,1)S(1)} all-gather(bf16[1,24,2]{1,2,0:T(2,128)(2,1)S(1)} %bitcast.442), channel_id=1, replica_groups=mesh['gx'=8,'gy'=4] {'gx','gy'}, dimensions={0}, use_global_device_ids=true | all-gather | bytes 3168 | tf_op jit(solution)/shard_map/all_gather | solution.py:159
  230.9 37.8 %all-gather.4 = bf16[32,24,2]{1,2,0:T(2,128)(2,1)S(1)} all-gather(bf16[1,24,2]{1,2,0:T(2,128)(2,1)S(1)} %bitcast.443), channel_id=1, replica_groups=mesh['gx'=8,'gy'=4] {'gx','gy'}, dimensions={0}, use_global_device_ids=true | all-gather | bytes 3168 | tf_op jit(solution)/shard_map/all_gather | solution.py:160
  268.8 36.4 %all-gather.5 = bf16[32,24,2]{1,2,0:T(2,128)(2,1)S(1)} all-gather(bf16[1,24,2]{1,2,0:T(2,128)(2,1)S(1)} %bitcast.444), channel_id=1, replica_groups=mesh['gx'=8,'gy'=4] {'gx','gy'}, dimensions={0}, use_global_device_ids=true | all-gather | bytes 3168 | tf_op jit(solution)/shard_map/all_gather | solution.py:161
  305.4 38.2 %all-gather.6 = bf16[32,24,2]{1,2,0:T(2,128)(2,1)S(1)} all-gather(bf16[1,24,2]{1,2,0:T(2,128)(2,1)S(1)} %bitcast.445), channel_id=1, replica_groups=mesh['gx'=8,'gy'=4] {'gx','gy'}, dimensions={0}, use_global_device_ids=true | all-gather | bytes 3168 | tf_op jit(solution)/shard_map/all_gather | solution.py:162
  353.4 50.3 %while.56 = (s32[]{:T(128)}, bf16[6,432,128]{1,2,0:T(8,128)(2,1)S(1)}, f32[6,2,432,1]{2,1,3,0:T(2,128)S(1)}, s32[6]{0:T(128)S(1)}, bf16[1728,768]{0,1:T(8,128)(2...) while((s32[]{:T(128)}, ...), condition=%wide.region_5.6_spmd.clone, body=%wide.region_2.5_spmd.clone.sunk | while | flops 399374496 | bytes 24299664 | solution.py:73
  409.6 37.0 %all-gather.7 = bf16[32,96,2]{1,2,0:T(2,128)(2,1)S(1)} all-gather(bf16[1,96,2]{1,2,0:T(2,128)(2,1)S(1)} %bitcast.446), channel_id=1, replica_groups=mesh['gx'=8,'gy'=4] {'gx','gy'}, dimensions={0}, use_global_device_ids=true | all-gather | bytes 12672 | tf_op jit(solution)/shard_map/all_gather | solution.py:163
  446.9 16.2 fusion.24
  463.1 22.2 %all-gather.37.cloned.1.call-done = bf16[2,768,768]{1,2,0:T(8,128)(2,1)} async-done(((bf16[2,768,96]{1,2,0:T(8,128)(2,1)}), bf16[2,768,768]{1,2,0:T(8,128)(2,1)}) %all-gather.37.cloned.1.call-update) | async-done | bytes 2359312 | tf_op jit(solution)/shard_map/all_gather | solution.py:170
  485.3 5.9 convolution_convert_fusion.3
  491.8 38.8 %all-gather.8 = bf16[32,24,2]{1,2,0:T(2,128)(2,1)S(1)} all-gather(bf16[1,24,2]{1,2,0:T(2,128)(2,1)S(1)} %bitcast.447), channel_id=1, replica_groups=mesh['gx'=8,'gy'=4] {'gx','gy'}, dimensions={0}, use_global_device_ids=true | all-gather | bytes 3168 | tf_op jit(solution)/shard_map/all_gather | solution.py:164
  542.6 18.6 all-gather.41.cloned.1.call-done
  565.8 23.4 %all-gather.39.cloned.1.call-done = bf16[1728,768]{1,0:T(8,128)(2,1)} async-done(((bf16[432,768]{1,0:T(8,128)(2,1)}), bf16[1728,768]{1,0:T(8,128)(2,1)}) %all-gather.39.cloned.1.call-update) | async-done | bytes 2654224 | tf_op jit(solution)/shard_map/all_gather | solution.py:196
  593.9 50.3 %while.57 = (s32[]{:T(128)}, bf16[6,432,128]{1,2,0:T(8,128)(2,1)S(1)}, f32[6,2,432,1]{2,1,3,0:T(2,128)S(1)}, s32[6]{0:T(128)S(1)}, bf16[1728,768]{0,1:T(8,128)(2...) while((s32[]{:T(128)}, ...), condition=%wide.region_14.15_spmd.clone, body=%wide.region_11.14_spmd.clone.sunk | while | flops 399374496 | bytes 24299664 | solution.py:73
  649.7 24.9 %all-gather.43.cloned.1.call-done = bf16[1728,768]{1,0:T(8,128)(2,1)} async-done(((bf16[432,768]{1,0:T(8,128)(2,1)}), bf16[1728,768]{1,0:T(8,128)(2,1)}) %all-gather.43.cloned.1.call-update) | async-done | bytes 2654224 | tf_op jit(solution)/shard_map/all_gather | solution.py:211
  674.5 16.1 fusion.27
  690.6 11.3 all-gather.45.cloned.1.call-done
  702.0 8.2 convert_reduce_fusion
  715.6 5.9 convolution_convert_fusion.2
  721.8 28.8 %reduce-scatter.38.cloned.1.call-done = bf16[432,768]{1,0:T(8,128)(2,1)} async-done(((bf16[1728,768]{1,0:T(8,128)(2,1)}), bf16[432,768]{1,0:T(8,128)(2,1)}) %reduce-scatter.38.cloned.1.call-update) | async-done | bytes 663568 | tf_op jit(solution)/shard_map/reduce_scatter | solution.py:273
  752.8 35.0 %reduce-scatter.36.cloned.1.call-done = bf16[432,768]{1,0:T(8,128)(2,1)} async-done(((bf16[1728,768]{1,0:T(8,128)(2,1)}), bf16[432,768]{1,0:T(8,128)(2,1)}) %reduce-scatter.36.cloned.1.call-update) | async-done | bytes 663568 | tf_op jit(solution)/shard_map/reduce_scatter | solution.py:218
  798.4 80.3 %while.58 = (s32[]{:T(128)}, bf16[6,432,128]{1,2,0:T(8,128)(2,1)S(1)}, bf16[6,1728,128]{1,2,0:T(8,128)(2,1)}, bf16[6,1728,128]{1,2,0:T(8,128)(2,1)}, s32[6]{0:T(...) while((s32[]{:T(128)}, ...), condition=%wide.region_23.24_spmd.clone, body=%wide.region_21.23_spmd.clone.sunk | while | flops 970250368 | bytes 53571120 | solution.py:113
  888.8 29.9 %reduce-scatter.50.cloned.1.call-done = bf16[432,768]{1,0:T(8,128)(2,1)} async-done(((bf16[1728,768]{1,0:T(8,128)(2,1)}), bf16[432,768]{1,0:T(8,128)(2,1)}) %reduce-scatter.50.cloned.1.call-update) | async-done | bytes 663568
  920.0 35.9 %reduce-scatter.48.cloned.1.call-done = bf16[432,768]{1,0:T(8,128)(2,1)} async-done(((bf16[1728,768]{1,0:T(8,128)(2,1)}), bf16[432,768]{1,0:T(8,128)(2,1)}) %reduce-scatter.48.cloned.1.call-update) | async-done | bytes 663568
  958.2 5.5 multiply_reduce_fusion.2
  967.4 25.8 %all-gather.47.cloned.1.call-done = bf16[1728,768]{1,0:T(8,128)(2,1)} async-done(((bf16[432,768]{1,0:T(8,128)(2,1)}), bf16[1728,768]{1,0:T(8,128)(2,1)}) %all-gather.47.cloned.1.call-update) | async-done | bytes 2654224 | tf_op jit(solution)/shard_map/all_gather | solution.py:259
  993.3 7.7 convert_reduce_fusion.1
  1006.5 34.8 %reduce-scatter.40.cloned.1.call-done = bf16[432,768]{1,0:T(8,128)(2,1)} async-done(((bf16[1728,768]{1,0:T(8,128)(2,1)}), bf16[432,768]{1,0:T(8,128)(2,1)}) %reduce-scatter.40.cloned.1.call-update) | async-done | bytes 663568 | tf_op jit(solution)/shard_map/reduce_scatter | solution.py:273
  1049.7 79.0 %while.59 = (s32[]{:T(128)}, bf16[6,432,128]{1,2,0:T(8,128)(2,1)S(1)}, bf16[6,1728,128]{1,2,0:T(8,128)(2,1)}, bf16[6,1728,128]{1,2,0:T(8,128)(2,1)}, s32[6]{0:T(...) while((s32[]{:T(128)}, ...), condition=%wide.region_33.34_spmd.clone, body=%wide.region_31.33_spmd.clone.sunk | while | flops 970250368 | bytes 53571120 | solution.py:113
  1138.9 5.2 fusion.69
  1152.6 6.9 copy.100
  1159.6 5.1 fusion.67
  1176.1 30.1 %reduce-scatter.52.cloned.1.call-done = bf16[432,768]{1,0:T(8,128)(2,1)} async-done(((bf16[1728,768]{1,0:T(8,128)(2,1)}), bf16[432,768]{1,0:T(8,128)(2,1)}) %reduce-scatter.52.cloned.1.call-update) | async-done | bytes 663568
  1216.6 6.2 scatter_custom_fusion
  1222.8 5.4 copy.111
  1229.4 6.8 convolution_bitcast_fusion
  1236.2 5.3 convolution_bitcast_fusion.1
  1241.4 11.1 pad_maximum_fusion
  1255.0 53.5 %reduce-scatter.58.cloned.1.call-done = f32[96,2]{1,0:T(8,128)} async-done(((f32[3072,2]{1,0:T(8,128)}), f32[96,2]{1,0:T(8,128)}) %reduce-scatter.58.cloned.1.call-update) | async-done | bytes 784
  1310.0 109.9 %all-reduce.12.cloned.1.call-done = bf16[2,768,768]{1,0,2:T(2,128)(2,1)} async-done(((bf16[2,768,768]{1,0,2:T(2,128)(2,1)}), bf16[2,768,768]{1,0,2:T(2,128)(2,1)}) %all-reduce.12.cloned.1.call-update) | async-done | bytes 2359312
  1422.0 69.7 %reduce-scatter.46.cloned.1.call-done = bf16[2,96,768]{2,1,0:T(8,128)(2,1)} async-done(((bf16[2,768,768]{2,1,0:T(8,128)(2,1)}), bf16[2,96,768]{2,1,0:T(8,128)(2,1)}) %reduce-scatter.46.cloned.1.call-update) | async-done | bytes 294928 | tf_op jit(solution)/shard_map/reduce_scatter | solution.py:387
  1494.1 40.4 %all-reduce.9 = (f32[2,768]{1,0:T(2,128)S(1)}, f32[2,768]{1,0:T(2,128)S(1)}, f32[2,768]{1,0:T(2,128)S(1)}, f32[2,768]{1,0:T(2,128)S(1)}, f32[2,768]{1,0:T(2,128)...) all-reduce(f32[2,768]{1,0:T(2,128)S(1)} %pad_maximum_fusion.11, ...), channel_id=11, replica_groups=mesh['gx'=8,'gy'=4] {'gx','gy'}, use_global_device_ids=true, to_apply=%region_42.43.clone | all-reduce | flops 12288 | bytes 98304
  1539.6 65.1 %reduce-scatter.44.cloned.1.call-done = f32[2,24,768]{2,1,0:T(8,128)} async-done(((f32[2,768,768]{2,1,0:T(8,128)}), f32[2,24,768]{2,1,0:T(8,128)}) %reduce-scatter.44.cloned.1.call-update) | async-done | bytes 147472 | tf_op jit(solution)/shard_map/reduce_scatter | solution.py:380
  1604.8 109.1 %reduce-scatter.56.cloned.1.call-done = f32[24,1214]{1,0:T(8,128)} async-done(((f32[768,1214]{1,0:T(8,128)}), f32[24,1214]{1,0:T(8,128)}) %reduce-scatter.56.cloned.1.call-update) | async-done | bytes 116560
  1713.8 168.2 %reduce-scatter.42.cloned.1.call-done = f32[2,24,2304]{2,1,0:T(8,128)} async-done(((f32[2,768,2304]{2,1,0:T(8,128)}), f32[2,24,2304]{2,1,0:T(8,128)}) %reduce-scatter.42.cloned.1.call-update) | async-done | bytes 442384 | tf_op jit(solution)/shard_map/reduce_scatter | solution.py:377
  (705 shorter events, 408.2 us)
Async XLA Ops:
  7.2 82.3 %all-gather.23.cloned.1.call-start = ((), (), s32[]{:S(2)}) async-start(), calls=%async_computation.13 | async-start | bytes 2027520 | tf_op jit(solution)/shard_map/all_gather | solution.py:155
  7.9 136.3 %all-gather.25.cloned.1.call-start = ((), (), s32[]{:S(2)}) async-start(), calls=%async_computation.14 | async-start | bytes 7299072 | tf_op jit(solution)/shard_map/all_gather | solution.py:165
  8.7 335.5 %all-gather.29.cloned.1.call-start = ((), (), s32[]{:S(2)}) async-start(), calls=%async_computation.16 | async-start | bytes 3317760 | tf_op jit(solution)/shard_map/all_gather | solution.py:195
  89.5 54.8 %copy-start.55 = (f32[768]{0:T(1024)}, f32[768]{0:T(1024)S(1)}, u32[]{:S(2)}) copy-start(f32[768]{0:T(1024)S(1)} %get-tuple-element.683) | copy-start | bytes 9220
  89.5 54.8 %copy-start.68 = (f32[768]{0:T(1024)}, f32[768]{0:T(1024)S(1)}, u32[]{:S(2)}) copy-start(f32[768]{0:T(1024)S(1)} %get-tuple-element.531) | copy-start | bytes 9220
  89.5 443.0 %copy-start.57 = (f32[768]{0:T(1024)}, f32[768]{0:T(1024)S(1)}, u32[]{:S(2)}) copy-start(f32[768]{0:T(1024)S(1)} %get-tuple-element.684) | copy-start | bytes 9220
  89.5 443.0 %copy-start.70 = (f32[768]{0:T(1024)}, f32[768]{0:T(1024)S(1)}, u32[]{:S(2)}) copy-start(f32[768]{0:T(1024)S(1)} %get-tuple-element.530) | copy-start | bytes 9220
  94.3 310.6 %copy-start.8 = (bf16[432,768]{1,0:T(8,128)(2,1)}, bf16[432,768]{1,0:T(8,128)(2,1)S(1)}, u32[]{:S(2)}) copy-start(bf16[432,768]{1,0:T(8,128)(2,1)S(1)} %gather_fusion) | copy-start | bytes 1990660
  94.6 53.6 %copy-start.45 = (f32[432]{0:T(512)}, f32[432]{0:T(512)S(1)}, u32[]{:S(2)}) copy-start(f32[432]{0:T(512)S(1)} %broadcast_multiply_fusion.3) | copy-start | bytes 5188
  95.0 53.2 %copy-start.49 = (f32[432]{0:T(512)}, f32[432]{0:T(512)S(1)}, u32[]{:S(2)}) copy-start(f32[432]{0:T(512)S(1)} %multiply_reduce_fusion.9) | copy-start | bytes 5188
  95.0 53.2 %copy-start.64 = (f32[432]{0:T(512)}, f32[432]{0:T(512)S(1)}, u32[]{:S(2)}) copy-start(f32[432]{0:T(512)S(1)} %fusion.100) | copy-start | bytes 5188
  151.2 79.7 %copy-start.79 = (bf16[2,24]{1,0:T(2,128)(2,1)S(1)}, bf16[2,24]{1,0:T(2,128)(2,1)}, u32[]{:S(2)}) copy-start(bf16[2,24]{1,0:T(2,128)(2,1)} %param.34) | copy-start | bytes 292
  151.2 117.7 %copy-start.80 = (bf16[2,24]{1,0:T(2,128)(2,1)S(1)}, bf16[2,24]{1,0:T(2,128)(2,1)}, u32[]{:S(2)}) copy-start(bf16[2,24]{1,0:T(2,128)(2,1)} %param.35) | copy-start | bytes 292
  151.2 197.6 %all-gather.27.cloned.1.call-start = ((), (), s32[]{:S(2)}) async-start(), calls=%async_computation.15 | async-start | bytes 3317760 | tf_op jit(solution)/shard_map/all_gather | solution.py:196
  226.7 78.8 %copy-start.81 = (bf16[2,24]{1,0:T(2,128)(2,1)S(1)}, bf16[2,24]{1,0:T(2,128)(2,1)}, u32[]{:S(2)}) copy-start(bf16[2,24]{1,0:T(2,128)(2,1)} %param.36) | copy-start | bytes 292
  226.8 117.0 %copy-start.17 = (s32[1728]{0:T(1024)S(1)}, s32[1728]{0:T(1024)}, u32[]{:S(2)}) copy-start(s32[1728]{0:T(1024)} %param.27) | copy-start | bytes 20740
  229.6 174.1 %all-gather.31.cloned.1.call-start = ((), (), s32[]{:S(2)}) async-start(), calls=%async_computation.17 | async-start | bytes 2433024 | tf_op jit(solution)/shard_map/all_gather | solution.py:166
  230.2 216.7 %all-gather.35.cloned.1.call-start = ((), (), s32[]{:S(2)}) async-start(), calls=%async_computation.19 | async-start | bytes 2654208 | tf_op jit(solution)/shard_map/all_gather | solution.py:169
  230.8 216.1 %all-gather.33.cloned.1.call-start = ((), (), s32[]{:S(2)}) async-start(), calls=%async_computation.18 | async-start | bytes 3317760 | tf_op jit(solution)/shard_map/all_gather | solution.py:211
  305.4 102.3 %copy-start.39 = (f32[768]{0:T(1024)}, f32[768]{0:T(1024)S(1)}, u32[]{:S(2)}) copy-start(f32[768]{0:T(1024)S(1)} %get-tuple-element.519) | copy-start | bytes 9220
  407.3 123.5 %copy-start = (f32[432,768]{1,0:T(8,128)}, f32[432,768]{1,0:T(8,128)S(1)}, u32[]{:S(2)}) copy-start(f32[432,768]{1,0:T(8,128)S(1)} %get-tuple-element.670) | copy-start | bytes 3981316
  407.3 55.7 %copy-start.41 = (f32[432]{0:T(512)}, f32[432]{0:T(512)S(1)}, u32[]{:S(2)}) copy-start(f32[432]{0:T(512)S(1)} %broadcast_multiply_fusion.2) | copy-start | bytes 5188
  407.7 55.4 %copy-start.43 = (f32[432]{0:T(512)}, f32[432]{0:T(512)S(1)}, u32[]{:S(2)}) copy-start(f32[432]{0:T(512)S(1)} %fusion.101) | copy-start | bytes 5188
  408.8 76.4 %all-gather.37.cloned.1.call-start = ((), (), s32[]{:S(2)}) async-start(), calls=%async_computation.20 | async-start | bytes 2654208 | tf_op jit(solution)/shard_map/all_gather | solution.py:170
  409.6 121.2 %reduce-scatter.34.cloned.1.call-start = ((), (), s32[]{:S(2)}) async-start(), calls=%async_computation.21 | async-start | bytes 3317760 | tf_op jit(solution)/shard_map/reduce_scatter | solution.py:218
  491.2 70.0 %all-gather.41.cloned.1.call-start = ((), (), s32[]{:S(2)}) async-start(), calls=%async_computation.23 | async-start | bytes 3317760 | tf_op jit(solution)/shard_map/all_gather | solution.py:195
  539.2 50.0 %all-gather.39.cloned.1.call-start = ((), (), s32[]{:S(2)}) async-start(), calls=%async_computation.22 | async-start | bytes 3317760 | tf_op jit(solution)/shard_map/all_gather | solution.py:196
  542.1 132.5 %all-gather.43.cloned.1.call-start = ((), (), s32[]{:S(2)}) async-start(), calls=%async_computation.24 | async-start | bytes 3317760 | tf_op jit(solution)/shard_map/all_gather | solution.py:211
  648.6 53.3 %all-gather.45.cloned.1.call-start = ((), (), s32[]{:S(2)}) async-start(), calls=%async_computation.26 | async-start | bytes 3317760 | tf_op jit(solution)/shard_map/all_gather | solution.py:259
  649.4 101.2 %reduce-scatter.38.cloned.1.call-start = ((), (), s32[]{:S(2)}) async-start(), calls=%async_computation.27 | async-start | bytes 3317760 | tf_op jit(solution)/shard_map/reduce_scatter | solution.py:273
  715.5 72.3 %reduce-scatter.36.cloned.1.call-start = ((), (), s32[]{:S(2)}) async-start(), calls=%async_computation.25 | async-start | bytes 3317760 | tf_op jit(solution)/shard_map/reduce_scatter | solution.py:218
  721.5 197.2 %reduce-scatter.50.cloned.1.call-start = ((), (), s32[]{:S(2)}) async-start(), calls=%async_computation.34 | async-start | bytes 3317760
  883.6 72.3 %reduce-scatter.48.cloned.1.call-start = ((), (), s32[]{:S(2)}) async-start(), calls=%async_computation.33 | async-start | bytes 3317760
  888.2 70.0 %copy-start.48 = (f32[432]{0:T(512)S(1)}, f32[432]{0:T(512)}, u32[]{:S(2)}) copy-start(f32[432]{0:T(512)} %copy-done.47) | copy-start | bytes 5188
  888.3 70.0 %copy-start.58 = (f32[768]{0:T(1024)S(1)}, f32[768]{0:T(1024)}, u32[]{:S(2)}) copy-start(f32[768]{0:T(1024)} %copy-done.57) | copy-start | bytes 9220
  888.3 70.0 %copy-start.67 = (f32[432]{0:T(512)S(1)}, f32[432]{0:T(512)}, u32[]{:S(2)}) copy-start(f32[432]{0:T(512)} %copy-done.66) | copy-start | bytes 5188
  888.3 105.0 %all-gather.47.cloned.1.call-start = ((), (), s32[]{:S(2)}) async-start(), calls=%async_computation.28 | async-start | bytes 3317760 | tf_op jit(solution)/shard_map/all_gather | solution.py:259
  967.4 73.9 %reduce-scatter.40.cloned.1.call-start = ((), (), s32[]{:S(2)}) async-start(), calls=%async_computation.29 | async-start | bytes 3317760 | tf_op jit(solution)/shard_map/reduce_scatter | solution.py:273
  1006.3 168.5 %reduce-scatter.54.cloned.1.call-start = ((), (), s32[]{:S(2)}) async-start(), calls=%async_computation.36 | async-start | bytes 3317760
  1133.6 72.6 %reduce-scatter.52.cloned.1.call-start = ((), (), s32[]{:S(2)}) async-start(), calls=%async_computation.35 | async-start | bytes 3317760
  1138.3 170.3 %reduce-scatter.58.cloned.1.call-start = ((), (), s32[]{:S(2)}) async-start(), calls=%async_computation.38 | async-start | bytes 1622016
  1145.8 274.1 %all-reduce.12.cloned.1.call-start = ((), (), s32[]{:S(2)}) async-start(), calls=%async_computation.39 | async-start | bytes 4718592
  1159.5 332.2 %reduce-scatter.46.cloned.1.call-start = ((), (), s32[]{:S(2)}) async-start(), calls=%async_computation.32 | async-start | bytes 2654208 | tf_op jit(solution)/shard_map/reduce_scatter | solution.py:387
  1168.9 435.9 %reduce-scatter.44.cloned.1.call-start = ((), (), s32[]{:S(2)}) async-start(), calls=%async_computation.31 | async-start | bytes 4866048 | tf_op jit(solution)/shard_map/reduce_scatter | solution.py:380
  1174.3 539.6 %reduce-scatter.56.cloned.1.call-start = ((), (), s32[]{:S(2)}) async-start(), calls=%async_computation.37 | async-start | bytes 4055040
  1228.2 653.8 %reduce-scatter.42.cloned.1.call-start = ((), (), s32[]{:S(2)}) async-start(), calls=%async_computation.30 | async-start | bytes 14598144 | tf_op jit(solution)/shard_map/reduce_scatter | solution.py:377
  1252.6 240.9 %copy-start.27 = (bf16[6,432,128]{1,2,0:T(8,128)(2,1)S(1)}, bf16[6,432,128]{1,2,0:T(8,128)(2,1)}, u32[]{:S(2)}) copy-start(bf16[6,432,128]{1,2,0:T(8,128)(2,1)} %copy-done.25) | copy-start | bytes 1990660
  1254.5 239.3 %copy-start.22 = (bf16[432,768]{0,1:T(8,128)(2,1)S(1)}, bf16[432,768]{0,1:T(8,128)(2,1)}, u32[]{:S(2)}) copy-start(bf16[432,768]{0,1:T(8,128)(2,1)} %copy-done.20) | copy-start | bytes 1990660
  (70 other events, 729.5 us)
Sparse Core Ops, SparseCore 0:
  10.9 58.8 all-gather.22
  72.7 71.5 all-gather.24
  151.3 24.3 all-gather.28
  229.7 23.3 all-gather.26
  255.8 57.3 all-gather.30
  315.2 51.0 all-gather.34
  409.0 21.9 all-gather.32
  433.2 52.0 all-gather.36
  491.3 33.4 reduce-scatter.33
  539.4 21.8 all-gather.40
  563.4 25.7 all-gather.38
  648.8 25.7 all-gather.42
  676.2 25.7 all-gather.44
  715.7 34.8 reduce-scatter.37
  753.0 34.8 reduce-scatter.35
  883.8 34.8 reduce-scatter.49
  921.1 34.8 reduce-scatter.47
  967.5 25.7 all-gather.46
  1006.4 34.8 reduce-scatter.39
  1133.7 34.8 reduce-scatter.53
  1171.4 34.8 reduce-scatter.51
  1211.5 97.0 reduce-scatter.57
  1312.2 107.7 all-reduce.11
  1423.7 67.9 reduce-scatter.45
  1498.7 106.0 reduce-scatter.43
  1610.6 103.1 reduce-scatter.55
  1720.3 161.7 reduce-scatter.41
where the time goes:
time: 1900 us; the launch traced here: 1890 us
  waiting for transfers between devices  950 us (50%)
  blocking collectives  384 us (20%)
  matrix products  237 us (12%)
  local copies, waits for them, and re-layouts  186 us (10%)
  other arithmetic  95.4 us (5%)
    unnamed x34, waiting for transfers between devices  373 us
    reduce_scatter x1, waiting for transfers between devices, shards(): lax.psum_scatter(stacked_member(collected, 9), ('gx', 'gy'), scatter_dime...  168 us
    unnamed x220, local copies, waits for them, and re-layouts  76.2 us
    reduce_scatter x1, waiting for transfers between devices, shards(): lax.psum_scatter(up_stack.astype(jnp.bfloat16), 'gx', scatter_dimension=1...  69.7 us
    reduce_scatter x1, waiting for transfers between devices, shards(): lax.psum_scatter(stacked_member(collected, 10), ('gx', 'gy'), scatter_dim...  65.1 us
    reduce_scatter x2, waiting for transfers between devices, shards(): lax.psum_scatter(rows_grad.astype(jnp.bfloat16), 'gy', scatter_dimension=...  63.6 us
    dynamic_slice x84, local copies, waits for them, and re-layouts, column_pair(): lax.dynamic_slice_in_dim(matrix, pair_index * pair_width, pair_width, 1)  58.2 us
    dot_general x24, matrix products, pair_scores(): jnp.einsum('qhd,khd->hqk', head_query, head_keys, preferred_element_type=...  49.5 us
  transfers between devices with their start and end apart: 27, of which 19 were waited for; matrix products, arithmetic and copies ran while one was open for 12% of the time, Pallas kernels for 0%

commit v1 on v0

--- a/solution.py
+++ b/solution.py
@@ -1,8 +1,11 @@
+import functools
 import math
 
 import jax
 import jax.numpy as jnp
 from jax import lax
+from jax.experimental import pallas as pl
+from jax.experimental.pallas import tpu as pltpu
 from jax.sharding import PartitionSpec as P
 
 HEAD_DIM = 64
@@ -411,9 +414,762 @@
     )
 
 
+LOG2_E = 1.0 / math.log(2.0)
+LANES = 128
+BF16 = jnp.bfloat16
+F32 = jnp.float32
+MESH_ID = pl.DeviceIdType.MESH
+VMEM_LIMIT = 60 * 1024 * 1024
+
+
+def dot_nn(left, right):
+    return lax.dot_general(left, right, (((1,), (0,)), ((), ())), preferred_element_type=F32)
+
+
+def dot_nt(left, right):
+    return lax.dot_general(left, right, (((1,), (1,)), ((), ())), preferred_element_type=F32)
+
+
+def dot_tn(left, right):
+    return lax.dot_general(left, right, (((0,), (0,)), ((), ())), preferred_element_type=F32)
+
+
+def my_place():
+    gx = lax.axis_index("gx")
+    gy = lax.axis_index("gy")
+    return gx // 2, lax.rem(gx, 2), gy // 2, lax.rem(gy, 2)
+
+
+def device_at(z, x, y, core):
+    return (z * 2 + x, y * 2 + core)
+
+
+def flip_pairs(flip_y, flip_core):
+    pairs = []
+    for index in range(32):
+        gx, gy = divmod(index, 4)
+        pairs.append((index, gx * 4 + (gy ^ (2 * flip_y + flip_core))))
+    return pairs
+
+
+def to_partner(value):
+    return lax.ppermute(value, ("gx", "gy"), flip_pairs(1, 0))
+
+
+def to_sibling(value):
+    return lax.ppermute(value, ("gx", "gy"), flip_pairs(0, 1))
+
+
+def greet(place):
+    z, x, y, core = place
+    barrier = pltpu.get_barrier_semaphore()
+    others = [device_at(lax.rem(z + k, 4), x, y, core) for k in (1, 2, 3)]
+    others += [device_at(z, 1 - x, y, core), device_at(z, x, 1 - y, core)]
+    others += [device_at(z, x, y, 1 - core)]
+    for other in others:
+        pl.semaphore_signal(barrier, inc=1, device_id=other, device_id_type=MESH_ID)
+    pl.semaphore_wait(barrier, len(others))
+
+
+def remote(src, dst, send_sem, recv_sem, device):
+    return pltpu.make_async_remote_copy(
+        src_ref=src,
+        dst_ref=dst,
+        send_sem=send_sem,
+        recv_sem=recv_sem,
+        device_id=device,
+        device_id_type=MESH_ID,
+    )
+
+
+def gather_steps(place, shard, full, half, send, recv, local_sem):
+    z, x, y, core = place
+    rows = shard.shape[0]
+    low, high = pl.ds(0, half), pl.ds(half, rows - half)
+    keep = pltpu.make_async_copy(shard, full.at[z, x, y, core], local_sem)
+    along_z = [
+        remote(
+            shard,
+            full.at[z, x, y, core],
+            send.at[k - 1],
+            recv.at[k - 1],
+            device_at(lax.rem(z + k, 4), x, y, core),
+        )
+        for k in (1, 2, 3)
+    ]
+
+    def same(ref, slot, device):
+        return remote(ref, ref, send.at[slot], recv.at[slot], device)
+
+    to_x = device_at(z, 1 - x, y, core)
+    to_y = device_at(z, x, 1 - y, core)
+    first = [
+        same(full.at[:, x, y, core, low], 3, to_x),
+        same(full.at[:, x, y, core, high], 4, to_y),
+    ]
+    second = [
+        same(full.at[:, :, y, core, low], 5, to_y),
+        same(full.at[:, x, :, core, high], 6, to_x),
+    ]
+    third = [same(full.at[:, :, :, core], 7, device_at(z, x, y, 1 - core))]
+    return keep, along_z, first, second, third
+
+
+def gather_kernel(halves, *refs):
+    count = len(halves)
+    shards = refs[:count]
+    fulls = refs[count : 2 * count]
+    send, recv, local = refs[2 * count :]
+    place = my_place()
+    plans = [
+        gather_steps(place, shards[g], fulls[g], halves[g], send.at[g], recv.at[g], local.at[g])
+        for g in range(count)
+    ]
+
+    def start_z(g):
+        if g < count:
+            keep, along_z = plans[g][:2]
+            keep.start()
+            for copy in along_z:
+                copy.start()
+
+    def start_first(g):
+        if g < count:
+            keep, along_z, first = plans[g][:3]
+            keep.wait()
+            for copy in along_z:
+                copy.wait_recv()
+            for copy in first:
+                copy.start()
+
+    def start_second(g):
+        for copy in plans[g][2]:
+            copy.wait_recv()
+        for copy in plans[g][3]:
+            copy.start()
+
+    def start_third(g):
+        for copy in plans[g][3]:
+            copy.wait_recv()
+        for copy in plans[g][4]:
+            copy.start()
+
+    greet(place)
+    start_z(0)
+    start_z(1)
+    start_first(0)
+    for g in range(count):
+        start_z(g + 2)
+        start_second(g)
+        start_first(g + 1)
+        start_third(g)
+    for g in range(count):
+        keep, along_z, first, second, third = plans[g]
+        for copy in third:
+            copy.wait_recv()
+        for copy in along_z + first + second + third:
+            copy.wait_send()
+
+
+def gather_weights(shards, collective_id):
+    count = len(shards)
+    halves = tuple(shard.shape[0] // 2 for shard in shards)
+    return pl.pallas_call(
+        functools.partial(gather_kernel, halves),
+        out_shape=[jax.ShapeDtypeStruct((4, 2, 2, 2) + shard.shape, BF16) for shard in shards],
+        in_specs=[pl.BlockSpec(memory_space=pl.ANY)] * count,
+        out_specs=[pl.BlockSpec(memory_space=pl.ANY)] * count,
+        scratch_shapes=[
+            pltpu.SemaphoreType.DMA((count, 8)),
+            pltpu.SemaphoreType.DMA((count, 8)),
+            pltpu.SemaphoreType.DMA((count,)),
+        ],
+        compiler_params=pltpu.CompilerParams(collective_id=collective_id, has_side_effects=True),
+        name="gather_weights",
+    )(*shards)
+
+
+def reduce_kernel(shapes, *refs):
+    count = len(shapes)
+    parts = refs[:count]
+    outs = refs[count : 2 * count]
+    buffers = refs[2 * count : 2 * count + 6 * count]
+    send, recv, local = refs[2 * count + 6 * count :]
+    place = my_place()
+    z, x, y, core = place
+    to_x = device_at(z, 1 - x, y, core)
+    to_y = device_at(z, x, 1 - y, core)
+    to_core = device_at(z, x, y, 1 - core)
+    plans = []
+    for g, (rows, columns) in enumerate(shapes):
+        half = rows // 2
+        low, high = pl.ds(0, half), pl.ds(half, half)
+        own, from_core, second_a, second_b, third, fourth = buffers[6 * g : 6 * g + 6]
+
+        def send_to(src, dst, slot, device, g=g):
+            return remote(src, dst, send.at[g, slot], recv.at[g, slot], device)
+
+        plans.append(
+            (
+                pltpu.make_async_copy(parts[g].at[:, :, :, core], own, local.at[g]),
+                [send_to(parts[g].at[:, :, :, 1 - core], from_core, 0, to_core)],
+                [
+                    send_to(own.at[:, :, 1 - y, low], second_a, 1, to_y),
+                    send_to(own.at[:, 1 - x, :, high], second_b, 2, to_x),
+                ],
+                [
+                    send_to(own.at[:, 1 - x, y, low], third.at[0], 3, to_x),
+                    send_to(own.at[:, x, 1 - y, high], third.at[1], 4, to_y),
+                ],
+                [
+                    send_to(
+                        own.at[lax.rem(z + k, 4), x, y],
+                        fourth.at[k - 1],
+                        4 + k,
+                        device_at(lax.rem(z + k, 4), x, y, core),
+                    )
+                    for k in (1, 2, 3)
+                ],
+            )
+        )
+
+    def added(left, right):
+        return (left.astype(F32) + right.astype(F32)).astype(BF16)
+
+    def start_core(g):
+        if g < count:
+            plans[g][0].start()
+            for copy in plans[g][1]:
+                copy.start()
+
+    def start_second(g):
+        if g >= count:
+            return
+        own, from_core = buffers[6 * g : 6 * g + 2]
+        plans[g][0].wait()
+        for copy in plans[g][1]:
+            copy.wait_recv()
+
+        def add_one(i, carry):
+            a, b, c = i // 4, lax.rem(i // 2, 2), lax.rem(i, 2)
+            own[a, b, c] = added(own[a, b, c], from_core[a, b, c])
+            return carry
+
+        lax.fori_loop(0, 16, add_one, 0)
+        for copy in plans[g][2]:
+            copy.start()
+
+    def start_third(g):
+        rows = shapes[g][0]
+        half = rows // 2
+        low, high = pl.ds(0, half), pl.ds(half, half)
+        own, unused, second_a, second_b = buffers[6 * g : 6 * g + 4]
+        for copy in plans[g][2]:
+            copy.wait_recv()
+
+        def add_one(i, carry):
+            a, b = i // 2, lax.rem(i, 2)
+            own[a, b, y, low] = added(own[a, b, y, low], second_a[a, b])
+            own[a, x, b, high] = added(own[a, x, b, high], second_b[a, b])
+            return carry
+
+        lax.fori_loop(0, 8, add_one, 0)
+        for copy in plans[g][3]:
+            copy.start()
+
+    def start_fourth(g):
+        rows = shapes[g][0]
+        half = rows // 2
+        low, high = pl.ds(0, half), pl.ds(half, half)
+        own, third = buffers[6 * g], buffers[6 * g + 4]
+        for copy in plans[g][3]:
+            copy.wait_recv()
+
+        def add_one(a, carry):
+            own[a, x, y, low] = added(own[a, x, y, low], third[0, a])
+            own[a, x, y, high] = added(own[a, x, y, high], third[1, a])
+            return carry
+
+        lax.fori_loop(0, 4, add_one, 0)
+        for copy in plans[g][4]:
+            copy.start()
+
+    def finish(g):
+        own, fourth = buffers[6 * g], buffers[6 * g + 5]
+        for copy in plans[g][4]:
+            copy.wait_recv()
+        total = own[z, x, y].astype(F32)
+        for k in range(3):
+            total = total + fourth[k].astype(F32)
+        outs[g][...] = total
+
+    greet(place)
+    start_core(0)
+    start_core(1)
+    start_second(0)
+    for g in range(count):
+        start_core(g + 2)
+        start_third(g)
+        start_second(g + 1)
+        start_fourth(g)
+        if g > 0:
+            finish(g - 1)
+    finish(count - 1)
+    for g in range(count):
+        for copies in plans[g][1:]:
+            for copy in copies:
+                copy.wait_send()
+
+
+def reduce_weights(parts, collective_id):
+    count = len(parts)
+    shapes = tuple(part.shape[-2:] for part in parts)
+    scratch = []
+    for rows, columns in shapes:
+        half = rows // 2
+        scratch += [
+            pltpu.VMEM((4, 2, 2, rows, columns), BF16),
+            pltpu.VMEM((4, 2, 2, rows, columns), BF16),
+            pltpu.VMEM((4, 2, half, columns), BF16),
+            pltpu.VMEM((4, 2, half, columns), BF16),
+            pltpu.VMEM((2, 4, half, columns), BF16),
+            pltpu.VMEM((3, rows, columns), BF16),
+        ]
+    return pl.pallas_call(
+        functools.partial(reduce_kernel, shapes),
+        out_shape=[jax.ShapeDtypeStruct(shape, F32) for shape in shapes],
+        in_specs=[pl.BlockSpec(memory_space=pl.ANY)] * count,
+        out_specs=[pl.BlockSpec(memory_space=pltpu.VMEM)] * count,
+        scratch_shapes=scratch
+        + [
+            pltpu.SemaphoreType.DMA((count, 8)),
+            pltpu.SemaphoreType.DMA((count, 8)),
+            pltpu.SemaphoreType.DMA((count,)),
+        ],
+        compiler_params=pltpu.CompilerParams(
+            collective_id=collective_id, has_side_effects=True, vmem_limit_bytes=VMEM_LIMIT
+        ),
+        name="reduce_weights",
+    )(*parts)
+
+
+def lane_marks(head):
+    lane = lax.broadcasted_iota(jnp.int32, (1, LANES), 1)
+    own = (lane // HEAD_DIM == head).astype(F32)
+    spare = HEAD_DIM * (1 - head)
+    return lane, own, spare
+
+
+def split_three(column):
+    high = column.astype(BF16).astype(F32)
+    rest = column - high
+    middle = rest.astype(BF16).astype(F32)
+    return high, middle, rest - middle
+
+
+def attention_kernel(block, q_ref, ko_ref, ks_ref, vo_ref, vs_ref, bias_ref, out_ref, exact_ref, lse_ref, keys, values):
+    pair = pl.program_id(0)
+    rows = q_ref.shape[0]
+    values[0:rows] = vo_ref[...]
+    values[rows:] = vs_ref[...]
+    lanes = lax.broadcasted_iota(jnp.int32, (1, LANES), 1)
+
+    @pl.when(pair == 0)
+    def _():
+        lse_ref[...] = jnp.zeros_like(lse_ref)
+
+    mixed = [[], []]
+    totals = [[], []]
+    for head in range(2):
+        lane, own, spare = lane_marks(head)
+        own16 = own.astype(BF16)
+        at_spare = (lane == spare).astype(BF16)
+        keys[0:rows] = ko_ref[...] * own16 + bias_ref[0:rows] * at_spare
+        keys[rows:] = ks_ref[...] * own16 + bias_ref[rows:] * at_spare
+        for start in range(0, rows, block):
+            query = q_ref[start : start + block] * own16 + at_spare
+            scores = dot_nt(query, keys[...])
+            top = jnp.max(scores, axis=-1, keepdims=True)
+            weights = jnp.exp2(scores - top)
+            total = jnp.sum(weights, axis=-1, keepdims=True)
+            summed = dot_nn(weights.astype(BF16), values[...])
+            mixed[head].append(summed * (1.0 / total))
+            totals[head].append(top + jnp.log2(total))
+    for index, start in enumerate(range(0, rows, block)):
+        rows_at = slice(start, start + block)
+        both = jnp.where(lanes < HEAD_DIM, mixed[0][index], mixed[1][index])
+        out_ref[rows_at] = both.astype(BF16)
+        exact_ref[rows_at] = both
+        held = lse_ref[rows_at]
+        held = jnp.where(lanes == 2 * pair, totals[0][index], held)
+        lse_ref[rows_at] = jnp.where(lanes == 2 * pair + 1, totals[1][index], held)
+
+
+def attention_forward(queries, keys_own, keys_sib, values_own, values_sib, bias):
+    rows, width = queries.shape
+    block = rows // 2
+    column = pl.BlockSpec((rows, LANES), lambda pair: (0, pair))
+    return pl.pallas_call(
+        functools.partial(attention_kernel, block),
+        grid=(width // LANES,),
+        out_shape=[
+            jax.ShapeDtypeStruct((rows, width), BF16),
+            jax.ShapeDtypeStruct((rows, width), F32),
+            jax.ShapeDtypeStruct((rows, LANES), F32),
+        ],
+        in_specs=[column] * 5 + [pl.BlockSpec((2 * rows, LANES), lambda pair: (0, 0))],
+        out_specs=[column, column, pl.BlockSpec((rows, LANES), lambda pair: (0, 0))],
+        scratch_shapes=[pltpu.VMEM((2 * rows, LANES), BF16), pltpu.VMEM((2 * rows, LANES), BF16)],
+        compiler_params=pltpu.CompilerParams(vmem_limit_bytes=VMEM_LIMIT),
+        cost_estimate=pl.CostEstimate(
+            flops=8 * rows * 2 * rows * width, bytes_accessed=12 * rows * width, transcendentals=0
+        ),
+        name="attention_forward",
+    )(queries, keys_own, keys_sib, values_own, values_sib, bias)
+
+
+def attention_back_kernel(
+    q_ref, ko_ref, ks_ref, vo_ref, vs_ref, do_ref, mix_ref, lse_ref, bias_ref,
+    dq_ref, dko_ref, dks_ref, dvo_ref, dvs_ref,
+):
+    pair = pl.program_id(0)
+    rows = q_ref.shape[0]
+    block = rows // 2
+    lanes = lax.broadcasted_iota(jnp.int32, (1, LANES), 1)
+    query = q_ref[...]
+    grad = do_ref[...]
+    product = grad.astype(F32) * mix_ref[...]
+    heads = []
+    for head in range(2):
+        lane, own, spare = lane_marks(head)
+        own16 = own.astype(BF16)
+        lse = jnp.sum(jnp.where(lanes == 2 * pair + head, lse_ref[...], 0.0), axis=-1, keepdims=True)
+        inner = jnp.sum(product * own, axis=-1, keepdims=True)
+        lse_parts, inner_parts = split_three(-lse), split_three(-inner)
+        query_own = query * own16
+        grad_own = grad * own16
+        query_aug = jnp.where(lane == spare, 1.0, 0.0)
+        grad_aug = jnp.zeros((1, LANES), F32)
+        for k in range(3):
+            query_aug = jnp.where(lane == spare + 1 + k, lse_parts[k], query_aug)
+            grad_aug = jnp.where(lane == spare + 1 + k, inner_parts[k], grad_aug)
+        query_aug = query_own + query_aug.astype(BF16)
+        grad_aug = grad_own + grad_aug.astype(BF16)
+        at_spare = (lane == spare).astype(BF16)
+        ones = ((lane > spare) & (lane < spare + 4)).astype(BF16)
+        heads.append((own16, at_spare, ones, query_own, grad_own, query_aug, grad_aug))
+    query_grad = jnp.zeros((LANES, rows), F32)
+    for side, (k_ref, v_ref, dk_ref, dv_ref) in enumerate(
+        ((ko_ref, vo_ref, dko_ref, dvo_ref), (ks_ref, vs_ref, dks_ref, dvs_ref))
+    ):
+        for start in range(0, rows, block):
+            at = slice(start, start + block)
+            key, value = k_ref[at], v_ref[at]
+            shift = bias_ref[side * rows + start : side * rows + start + block]
+            key_grad = jnp.zeros((block, LANES), F32)
+            value_grad = jnp.zeros((block, LANES), F32)
+            for own16, at_spare, ones, query_own, grad_own, query_aug, grad_aug in heads:
+                key_own = key * own16
+                weights = jnp.exp2(dot_nt(key_own + shift * at_spare + ones, query_aug))
+                weight_grad = dot_nt(value * own16 + ones, grad_aug)
+                score_grad = (weights * weight_grad).astype(BF16)
+                value_grad = value_grad + dot_nn(weights.astype(BF16), grad_own)
+                key_grad = key_grad + dot_nn(score_grad, query_own)
+                query_grad = query_grad + dot_tn(key_own, score_grad)
+            dk_ref[at] = (key_grad * (1.0 / LOG2_E)).astype(BF16)
+            dv_ref[at] = value_grad.astype(BF16)
+    dq_ref[...] = (jnp.transpose(query_grad) * HEAD_DIM ** (-0.5)).astype(BF16)
+
+
+def attention_backward(queries, keys_own, keys_sib, values_own, values_sib, mixed_grad, mixed, lse, bias):
+    rows, width = queries.shape
+    column = pl.BlockSpec((rows, LANES), lambda pair: (0, pair))
+    fixed = pl.BlockSpec((rows, LANES), lambda pair: (0, 0))
+    return pl.pallas_call(
+        attention_back_kernel,
+        grid=(width // LANES,),
+        out_shape=[jax.ShapeDtypeStruct((rows, width), BF16)] * 5,
+        in_specs=[column] * 7 + [fixed, pl.BlockSpec((2 * rows, LANES), lambda pair: (0, 0))],
+        out_specs=[column] * 5,
+        compiler_params=pltpu.CompilerParams(vmem_limit_bytes=VMEM_LIMIT),
+        cost_estimate=pl.CostEstimate(
+            flops=20 * rows * 2 * rows * width, bytes_accessed=24 * rows * width, transcendentals=0
+        ),
+        name="attention_backward",
+    )(queries, keys_own, keys_sib, values_own, values_sib, mixed_grad, mixed, lse, bias)
+
+
+def norm_parts(values):
+    row_mean = jnp.mean(values, axis=-1, keepdims=True)
+    centred = values - row_mean
+    row_var = jnp.mean(centred * centred, axis=-1, keepdims=True)
+    rstd = lax.rsqrt(row_var + EPSILON)
+    return centred * rstd, rstd
+
+
+def norm_back(values, gain, grad):
+    normed, rstd = norm_parts(values)
+    scaled = grad * gain
+    first = jnp.mean(scaled, axis=-1, keepdims=True)
+    second = jnp.mean(scaled * normed, axis=-1, keepdims=True)
+    back = (scaled - first - normed * second) * rstd
+    return back, jnp.sum(grad * normed, axis=0), jnp.sum(grad, axis=0)
+
+
+def split_rows(values):
+    high = values.astype(BF16)
+    rest = values - high.astype(F32)
+    middle = rest.astype(BF16)
+    return high, middle, (rest - middle.astype(F32)).astype(BF16)
+
+
+def chip_shards(
+    patches,
+    clip_of_row,
+    position_of_row,
+    pos_embed,
+    norm1_gain,
+    norm1_bias,
+    query_bias,
+    value_bias,
+    out_bias,
+    norm2_gain,
+    norm2_bias,
+    up_bias,
+    down_bias,
+    qkv_weight,
+    out_weight,
+    up_weight,
+    down_weight,
+    cotangent,
+):
+    layers, owned, features = qkv_weight.shape[0], qkv_weight.shape[1], patches.shape[1]
+    pieces = lax.axis_size("gy")
+    piece_rows = patches.shape[0]
+    devices = features // owned
+    positions = pos_embed.shape[0]
+    padded_positions = -(-positions // 256) * 256
+    slots = -(-positions // pieces)
+    slots = -(-slots // 16) * 16
+    rows = 2 * slots
+    hidden_width = up_weight.shape[2]
+    up_rows = up_weight.shape[1]
+    gy = lax.axis_index("gy")
+    side, core = gy // 2, lax.rem(gy, 2)
+
+    low_clip, high_clip = jnp.min(clip_of_row), jnp.max(clip_of_row)
+    low_is_long = 2 * jnp.sum((clip_of_row == low_clip).astype(jnp.int32)) > clip_of_row.shape[0]
+    long_clip = jnp.where(low_is_long, low_clip, high_clip)
+    kept_all = ((clip_of_row == long_clip) == (side == 0)).reshape(pieces, piece_rows)
+    kept_count = jnp.sum(kept_all.astype(jnp.int32), axis=1)
+    kept = lax.dynamic_index_in_dim(kept_all, gy, 0, keepdims=False)
+    rank_kept = jnp.cumsum(kept.astype(jnp.int32)) - 1
+    rank_sent = jnp.arange(piece_rows, dtype=jnp.int32) - rank_kept - 1
+    slot = jnp.arange(slots, dtype=jnp.int32)[:, None]
+    pick_kept = (slot == rank_kept[None]) & kept[None]
+    pick_sent = (slot == rank_sent[None]) & jnp.logical_not(kept)[None]
+    choose = jnp.concatenate([pick_kept, pick_sent], axis=0)
+    choose16 = choose.astype(BF16)
+    sorted_rows = dot_nn(choose16, jnp.concatenate([patches, cotangent], axis=1)).astype(BF16)
+    sorted_positions = jnp.sum(jnp.where(choose, position_of_row[None], 0), axis=1)
+    received = to_partner(sorted_rows[slots:])
+    received_positions = to_partner(sorted_positions[slots:])
+    own_rows = jnp.concatenate([sorted_rows[:slots], received], axis=0)
+    row_positions = jnp.concatenate([sorted_positions[:slots], received_positions])
+    chip_patches, chip_cotangent = own_rows[:, :features], own_rows[:, features:]
+
+    def slot_bias(of_core):
+        mine = lax.dynamic_index_in_dim(kept_count, side * 2 + of_core, 0, keepdims=False)
+        theirs = lax.dynamic_index_in_dim(kept_count, (1 - side) * 2 + of_core, 0, keepdims=False)
+        steps = jnp.arange(slots, dtype=jnp.int32)
+        used = jnp.concatenate([steps < mine, steps < theirs])
+        return jnp.where(used, 0.0, MASKED)
+
+    bias = jnp.concatenate([slot_bias(core), slot_bias(1 - core)]).astype(BF16)
+    bias = jnp.broadcast_to(bias[:, None], (2 * rows, LANES))
+
+    narrow = jnp.stack(
+        [norm1_gain, norm1_bias, query_bias, value_bias, out_bias, norm2_gain, norm2_bias, down_bias],
+        axis=1,
+    )
+    small = jnp.concatenate([narrow.reshape(-1), up_bias.reshape(-1)])
+    table_shard = jnp.concatenate(
+        [
+            jnp.pad(pos_embed.T, ((0, 0), (0, padded_positions - positions))),
+            jnp.pad(small[None], ((0, 7), (0, padded_positions - small.shape[0]))),
+        ],
+        axis=0,
+    )
+    shards = [table_shard]
+    for layer in range(layers):
+        qkv = jnp.transpose(qkv_weight[layer].reshape(owned, 3, features), (1, 0, 2))
+        shards.append(jnp.concatenate([qkv.reshape(3 * owned, features), out_weight[layer]], axis=0))
+        shards.append(jnp.concatenate([up_weight[layer], down_weight[layer].T], axis=0))
+    gathered = gather_weights(shards, 0)
+    table_all = gathered[0].reshape(devices, owned + 8, padded_positions)
+    table = table_all[:, :owned].reshape(features, padded_positions)
+    small_all = table_all[:, owned, : small.shape[0]].astype(F32)
+    count = narrow.shape[1]
+    split = layers * count * owned
+    narrow_all = jnp.transpose(
+        small_all[:, :split].reshape(devices, layers, count, owned), (1, 2, 0, 3)
+    ).reshape(layers, count, features)
+    up_bias_all = jnp.transpose(
+        small_all[:, split:].reshape(devices, layers, -1), (1, 0, 2)
+    ).reshape(layers, -1)
+
+    position_ids = jnp.arange(padded_positions, dtype=jnp.int32)
+    lookup = (row_positions[:, None] == position_ids[None]).astype(BF16)
+    state = chip_patches.astype(F32) + dot_nt(lookup, table)
+    score_scale = HEAD_DIM ** (-0.5) * LOG2_E
+
+    stored = []
+    for layer in range(layers):
+        gain_one, shift_one, bias_query, bias_value, bias_out, gain_two, shift_two, bias_down = (
+            narrow_all[layer, i] for i in range(count)
+        )
+        attn = gathered[1 + 2 * layer].reshape(devices, 4, owned, features)
+        weight_q, weight_k, weight_v, weight_o = (
+            attn[:, i].reshape(features, features) for i in range(4)
+        )
+        mlp = gathered[2 + 2 * layer].reshape(devices // pieces, pieces, 2, up_rows, hidden_width)
+        weight_up, weight_down = (
+            jnp.transpose(mlp[:, :, i], (0, 2, 1, 3)).reshape(features, pieces * hidden_width)
+            for i in range(2)
+        )
+        normed, unused = norm_parts(state)
+        act_one = (normed * gain_one + shift_one).astype(BF16)
+        queries = ((dot_nn(act_one, weight_q) + bias_query) * score_scale).astype(BF16)
+        key_rows = dot_nn(act_one, weight_k).astype(BF16)
+        value_rows = (dot_nn(act_one, weight_v) + bias_value).astype(BF16)
+        key_sib, value_sib = to_sibling(key_rows), to_sibling(value_rows)
+        mixed, exact, lse = attention_forward(queries, key_rows, key_sib, value_rows, value_sib, bias)
+        middle = state + dot_nn(mixed, weight_o) + bias_out
+        normed_two, unused = norm_parts(middle)
+        act_two = (normed_two * gain_two + shift_two).astype(BF16)
+        pre_act = dot_nn(act_two, weight_up) + up_bias_all[layer]
+        below = 0.5 * (1.0 + lax.erf(pre_act * SQRT_HALF))
+        hidden = (pre_act * below).astype(BF16)
+        slope = (below + pre_act * jnp.exp(-0.5 * pre_act * pre_act) * NORMAL_PEAK).astype(BF16)
+        layer_out = middle + dot_nn(hidden, weight_down.T) + bias_down
+        stored.append(
+            (state, act_one, queries, key_rows, key_sib, value_rows, value_sib, mixed, exact, lse, middle,
+             act_two, hidden, slope, weight_q, weight_k, weight_v, weight_o, weight_up, weight_down,
+             gain_one, gain_two)
+        )
+        state = layer_out
+
+    def from_chip(values_own, values_back):
+        both = jnp.concatenate([values_own, values_back], axis=0)
+        parts = split_rows(both)
+        return sum(dot_tn(choose16, part) for part in parts)
+
+    activations = from_chip(state[:slots], to_partner(state[slots:]))
+
+    def by_owner(part):
+        return part.reshape(devices, owned, part.shape[1])
+
+    def by_blocks(part):
+        return jnp.transpose(
+            part.reshape(devices // pieces, up_rows, pieces, hidden_width), (0, 2, 1, 3)
+        ).reshape(devices, up_rows, hidden_width)
+
+    gradient = chip_cotangent.astype(F32)
+    attn_parts, mlp_parts, narrow_parts, up_bias_parts = ([None] * layers for _ in range(4))
+    for layer in reversed(range(layers)):
+        (before, act_one, queries, key_rows, key_sib, value_rows, value_sib, mixed, exact, lse, middle,
+         act_two, hidden, slope, weight_q, weight_k, weight_v, weight_o, weight_up, weight_down,
+         gain_one, gain_two) = stored[layer]
+        grad_two = gradient.astype(BF16)
+        down_bias_part = jnp.sum(grad_two.astype(F32), axis=0)
+        down_part = dot_tn(grad_two, hidden)
+        pre_grad = (dot_nn(grad_two, weight_down) * slope.astype(F32)).astype(BF16)
+        up_part = dot_tn(act_two, pre_grad)
+        up_bias_parts[layer] = jnp.sum(pre_grad.astype(F32), axis=0)
+        act_two_grad = dot_nt(pre_grad, weight_up)
+        mlp_parts[layer] = jnp.concatenate([by_blocks(up_part), by_blocks(down_part)], axis=1).astype(BF16)
+        back_two, gain_two_part, shift_two_part = norm_back(middle, gain_two, act_two_grad)
+        mid_grad = gradient + back_two
+        grad_one = mid_grad.astype(BF16)
+        out_bias_part = jnp.sum(grad_one.astype(F32), axis=0)
+        out_part = dot_tn(mixed, grad_one)
+        mixed_grad = dot_nt(grad_one, weight_o).astype(BF16)
+        query_grad, key_own, key_far, value_own, value_far = attention_backward(
+            queries, key_rows, key_sib, value_rows, value_sib, mixed_grad, exact, lse, bias
+        )
+        key_grad = (key_own.astype(F32) + to_sibling(key_far).astype(F32)).astype(BF16)
+        value_grad = (value_own.astype(F32) + to_sibling(value_far).astype(F32)).astype(BF16)
+        query_bias_part = jnp.sum(query_grad.astype(F32), axis=0)
+        value_bias_part = jnp.sum(value_grad.astype(F32), axis=0)
+        attn_parts[layer] = jnp.concatenate(
+            [by_owner(dot_tn(act_one, g)) for g in (query_grad, key_grad, value_grad)]
+            + [by_owner(out_part)],
+            axis=1,
+        ).astype(BF16)
+        act_one_grad = (
+            dot_nt(query_grad, weight_q) + dot_nt(key_grad, weight_k) + dot_nt(value_grad, weight_v)
+        )
+        back_one, gain_one_part, shift_one_part = norm_back(before, gain_one, act_one_grad)
+        gradient = mid_grad + back_one
+        narrow_parts[layer] = jnp.stack(
+            [gain_one_part, shift_one_part, query_bias_part, value_bias_part, out_bias_part,
+             gain_two_part, shift_two_part, down_bias_part]
+        )
+    input_grad = from_chip(gradient[:slots], to_partner(gradient[slots:]))
+
+    table_part = dot_tn(gradient.astype(BF16), lookup)
+    narrow_part = jnp.transpose(
+        jnp.stack(narrow_parts).reshape(layers, count, devices, owned), (2, 0, 1, 3)
+    ).reshape(devices, split)
+    up_bias_part = jnp.transpose(
+        jnp.stack(up_bias_parts).reshape(layers, devices, -1), (1, 0, 2)
+    ).reshape(devices, -1)
+    small_part = jnp.concatenate([narrow_part, up_bias_part], axis=1)[:, None]
+    table_parts = jnp.concatenate(
+        [
+            by_owner(table_part),
+            jnp.pad(small_part, ((0, 0), (0, 7), (0, padded_positions - small_part.shape[2]))),
+        ],
+        axis=1,
+    ).astype(BF16)
+    grouped = []
+    for layer in reversed(range(layers)):
+        grouped += [mlp_parts[layer], attn_parts[layer]]
+    grouped.append(table_parts)
+    sums = reduce_weights([part.reshape((4, 2, 2, 2) + part.shape[1:]) for part in grouped], 1)
+    table_sum = sums[-1]
+    pos_embed_grad = table_sum[:owned, :positions].T
+    small_sum = table_sum[owned, : small.shape[0]]
+    narrow_sum = small_sum[:split].reshape(layers, count, owned)
+    up_bias_grad = small_sum[split:].reshape(layers, -1)
+    mlp_sums = sums[-3::-2]
+    attn_sums = sums[-2::-2]
+    qkv_weight_grad = jnp.stack(
+        [
+            jnp.transpose(part[: 3 * owned].reshape(3, owned, features), (1, 0, 2)).reshape(owned, -1)
+            for part in attn_sums
+        ]
+    )
+    out_weight_grad = jnp.stack([part[3 * owned :] for part in attn_sums])
+    up_weight_grad = jnp.stack([part[:up_rows] for part in mlp_sums])
+    down_weight_grad = jnp.stack([part[up_rows:].T for part in mlp_sums])
+    return (
+        activations,
+        input_grad,
+        pos_embed_grad,
+        *(narrow_sum[:, i] for i in range(7)),
+        up_bias_grad,
+        narrow_sum[:, 7],
+        qkv_weight_grad,
+        out_weight_grad,
+        up_weight_grad,
+        down_weight_grad,
+    )
+
+
 def solution(mesh):
     return jax.shard_map(
-        shards,
+        chip_shards if mesh.shape["gx"] == 8 and mesh.shape["gy"] == 4 else shards,
         mesh=mesh,
         in_specs=(
             P(("gx", "gy"), None),

time: 1900 us -> 800 us (0.42)
  waiting for transfers between devices: 950 us -> 9.22 us
  Pallas kernels: 0 us -> 436 us
  blocking collectives: 384 us -> 0 us
  matrix products: 237 us -> 139 us
  other arithmetic: 95.4 us -> 48.8 us
  local copies, waits for them, and re-layouts: 186 us -> 140 us
    pallas_call x0 -> x6, Pallas kernels: none -> 436 us  [the longest x1 168 us: reduce_weights(): pl.pallas_call(functools.partial(reduce_kernel, shapes), out_shape=[jax.S...]
    reduce_scatter x7 -> x0, waiting for transfers between devices: 402 us -> none  [the longest x1 168 us: shards(): lax.psum_scatter(stacked_member(collected, 9), ('gx', 'gy'), scatter_dime...]
    unnamed x34 -> x0, waiting for transfers between devices: 373 us -> none
    all_gather x9 -> x0, blocking collectives: 343 us -> none  [the longest x1 43.2 us: shards(): lax.all_gather(norm1_gain, ('gx', 'gy'), axis=1, tiled=True)]
    all_gather x13 -> x0, waiting for transfers between devices: 176 us -> none  [the longest x1 49.2 us: shards(): lax.all_gather(qkv_weight, ('gx', 'gy'), axis=1, tiled=True)]
    dot_general x108 -> x45, matrix products: 237 us -> 139 us  [the longest x15 55.2 us: dot_nn(): lax.dot_general(left, right, (((1,), (0,)), ((), ())), preferred_element_...]
    dynamic_slice x109 -> x1, local copies, waits for them, and re-layouts: 72.3 us -> 0.61 us  [slot_bias(): lax.dynamic_index_in_dim(kept_count, side * 2 + of_core, 0, keepdims=False)]
    reshape x8 -> x20, local copies, waits for them, and re-layouts: 0.03 us -> 60.4 us  [the longest x8 58.5 us: by_blocks(): part.reshape(devices // pieces, up_rows, pieces, hidden_width)]
  transfers between devices with their start and end apart: 27 -> 12, of which waited for: 19 -> 1; matrix products, arithmetic and copies ran while one was open for 12% -> 28% of each run, Pallas kernels for 0% -> 25%
where the time goes in v1:
time: 800 us; the launch traced here: 789 us
  Pallas kernels  436 us (54%)
  local copies, waits for them, and re-layouts  140 us (18%)
  matrix products  139 us (17%)
  other arithmetic  48.8 us (6%)
  starting transfers between devices  11.4 us (1%)
  waiting for transfers between devices  9.22 us (1%)
    pallas_call x1, Pallas kernels, reduce_weights(): pl.pallas_call(functools.partial(reduce_kernel, shapes), out_shape=[jax.S...  168 us
    pallas_call x1, Pallas kernels, gather_weights(): pl.pallas_call(functools.partial(gather_kernel, halves), out_shape=[jax.S...  158 us
    pallas_call x2, Pallas kernels, attention_backward(): pl.pallas_call(attention_back_kernel, grid=(width // LANES,), out_shape=[...  72.8 us
    reshape x8, local copies, waits for them, and re-layouts, by_blocks(): part.reshape(devices // pieces, up_rows, pieces, hidden_width)  58.5 us
    dot_general x15, matrix products, dot_nn(): lax.dot_general(left, right, (((1,), (0,)), ((), ())), preferred_element_...  55.2 us
    dot_general x19, matrix products, dot_tn(): lax.dot_general(left, right, (((0,), (0,)), ((), ())), preferred_element_...  54.5 us
    unnamed x228, local copies, waits for them, and re-layouts  39.9 us
    pallas_call x2, Pallas kernels, attention_forward(): pl.pallas_call(functools.partial(attention_kernel, block), grid=(width //...  36.5 us
  transfers between devices with their start and end apart: 12, of which 1 were waited for; matrix products, arithmetic and copies ran while one was open for 28% of the time, Pallas kernels for 25%

profile of v1, /device:TPU:0, one launch (start us, length us, event | category | flops | bytes accessed | tf_op | source)
XLA Modules:
  0.0 789.3 jit_solution(13814044921624593528)
XLA Ops:
  8.9 3.0 collective-permute-start.1
  18.9 157.8 %gather_weights.1 = (bf16[4,2,2,2,32,1280]{5,4,3,2,1,0:T(8,128)(2,1)}, bf16[4,2,2,2,96,768]{5,4,3,2,1,0:T(8,128)(2,1)}, bf16[4,2,2,2,192,768]{5,4,3,2,1,0:T(8,12...) custom-call(bf16[32,1280]{1,0:T(8,128)(2,1)} %fusion.40.refs_0_, ...), custom_call_target="tpu_custom_call" | custom-call | tf_op jit(solution)/shard_map/gather_weights/pallas_call | solution.py:577
  176.7 4.2 fusion.66
  184.9 8.3 %fusion.64 = (bf16[8,4,1,96,768]{4,3,2,1,0:T(8,128)(2,1)}, bf16[8,4,1,96,768]{4,3,2,1,0:T(8,128)(2,1)}) fusion(bf16[8,4,2,96,768]{4,3,2,1,0:T(8,128)(2,1)} %bitcast.238), kind=kLoop, calls=%fused_computation.259 | loop fusion | bytes 18874368 | tf_op jit(solution)/shard_map/slice | solution.py:1037
  204.7 6.3 copy.104
  211.0 3.2 copy.117
  214.3 3.6 copy.103
  217.9 3.2 copy.116
  226.9 18.3 %attention_forward.2 = (bf16[608,768]{1,0:T(8,128)(2,1)}, f32[608,768]{1,0:T(8,128)}, f32[608,128]{1,0:T(8,128)}) custom-call(bf16[608,768]{1,0:T(8,128)(2,1)} %multiply_convert_fusion.5.q_ref, bf16[608,768]{1,0:T(8,128)(2,1)} %convolution_convert_fusion.17.ko_ref, bf16[608,768]{1,0:T(8,128)(2,1)} %collective-permute-done.2.ks_ref, ...), custom_call_target="tpu_custom_call" | custom-call | flops 4542431232 | bytes 5603328 | tf_op jit(solution)/shard_map/attention_forward/pallas_call | solution.py:812
  248.1 8.5 %multiply_convert_fusion.3 = (bf16[608,3072]{1,0:T(8,128)(2,1)S(1)}, f32[608,3072]{1,0:T(8,128)}) fusion(f32[3072]{0:T(1024)S(1)} %add.317, bf16[768,3072]{1,0:T(8,128)(2,1)} %bitcast.243, f32[608,768]{1,0:T(8,128)S(1)} %get-tuple-element.163, f32[768]{0:T(1024)S(1)} %get-tuple-element.93, f32[768]{0:T(1024)S(1)} %get-tuple-element.94, ...), kind=kOutput, calls=%fused_computation.18 | convolution fusion | flops 2882445312 | bytes 17816320 | tf_op jit(solution)/shard_map/dot_general | solution.py:426
  256.7 3.2 fusion.76
  265.8 6.9 fusion.63
  272.6 6.0 copy.106
  278.6 3.2 copy.119
  281.8 3.8 copy.105
  285.7 3.2 copy.118
  291.7 3.4 multiply_convert_fusion.4.q_ref
  295.0 18.3 %attention_forward.3 = (bf16[608,768]{1,0:T(8,128)(2,1)}, f32[608,768]{1,0:T(8,128)}, f32[608,128]{1,0:T(8,128)}) custom-call(bf16[608,768]{1,0:T(8,128)(2,1)} %multiply_convert_fusion.4.q_ref, bf16[608,768]{1,0:T(8,128)(2,1)} %convolution_convert_fusion.16.ko_ref, bf16[608,768]{1,0:T(8,128)(2,1)} %collective-permute-done.4.ks_ref, ...), custom_call_target="tpu_custom_call" | custom-call | flops 4542431232 | bytes 5603328 | tf_op jit(solution)/shard_map/attention_forward/pallas_call | solution.py:812
  316.3 6.3 multiply_convert_fusion.2
  322.7 6.4 fusion.78
  329.1 3.5 multiply_reduce_fusion
  332.7 6.2 convolution_convert_fusion.3
  344.2 5.7 convolution_convert_fusion.2
  349.9 4.4 add_add_fusion.2
  354.3 36.5 %attention_backward.2 = (bf16[608,768]{1,0:T(8,128)(2,1)}, bf16[608,768]{1,0:T(8,128)(2,1)}, bf16[608,768]{1,0:T(8,128)(2,1)}, bf16[608,768]{1,0:T(8,128)(2,1)}, bf16[608,768]{1,0:T(8,128)(2,1)}) custom-call(bf16[608,768]{1,0:T(8,128)(2,1)} %multiply_convert_fusion.4.q_ref, bf16[608,768]{1,0:T(8,128)(2,1)} %convolution_convert_fusion.16.ko_ref, ...), custom_call_target="tpu_custom_call" | custom-call | flops 11356078080 | bytes 11206656 | tf_op jit(solution)/shard_map/attention_backward/pallas_call | solution.py:888
  390.8 3.9 fusion.80
  398.8 9.7 %reshape.410 = bf16[8,96,4,768]{3,2,1,0:T(4,128)(2,1)} reshape(bf16[768,3072]{1,0:T(8,128)(2,1)} %convolution_convert_fusion.3) | data formatting | bytes 9437184 | tf_op jit(solution)/shard_map/reshape | solution.py:1074
  408.6 5.5 copy.85
  415.8 9.7 %reshape.411 = bf16[8,96,4,768]{3,2,1,0:T(4,128)(2,1)} reshape(bf16[768,3072]{1,0:T(8,128)(2,1)} %convolution_convert_fusion.2) | data formatting | bytes 9437184 | tf_op jit(solution)/shard_map/reshape | solution.py:1074
  425.5 3.2 copy.86
  429.8 6.9 pad_maximum_fusion.refs_0_
  442.5 5.6 convolution_convert_fusion
  448.2 6.0 fusion.79
  454.2 3.5 multiply_reduce_fusion.2
  464.9 36.3 %attention_backward.3 = (bf16[608,768]{1,0:T(8,128)(2,1)}, bf16[608,768]{1,0:T(8,128)(2,1)}, bf16[608,768]{1,0:T(8,128)(2,1)}, bf16[608,768]{1,0:T(8,128)(2,1)}, bf16[608,768]{1,0:T(8,128)(2,1)}) custom-call(bf16[608,768]{1,0:T(8,128)(2,1)} %multiply_convert_fusion.5.q_ref, bf16[608,768]{1,0:T(8,128)(2,1)} %convolution_convert_fusion.17.ko_ref, ...), custom_call_target="tpu_custom_call" | custom-call | flops 11356078080 | bytes 11206656 | tf_op jit(solution)/shard_map/attention_backward/pallas_call | solution.py:888
  501.3 3.5 fusion.81
  514.1 6.5 convolution_convert_fusion.1
  524.5 3.1 fusion.16
  530.2 9.7 %reshape.413 = bf16[8,96,4,768]{3,2,1,0:T(4,128)(2,1)} reshape(bf16[768,3072]{1,0:T(8,128)(2,1)} %convolution_convert_fusion) | data formatting | bytes 9437184 | tf_op jit(solution)/shard_map/reshape | solution.py:1074
  539.9 5.5 copy.88
  545.4 9.7 %reshape.412 = bf16[8,96,4,768]{3,2,1,0:T(4,128)(2,1)} reshape(bf16[768,3072]{1,0:T(8,128)(2,1)} %convolution_convert_fusion.1) | data formatting | bytes 9437184 | tf_op jit(solution)/shard_map/reshape | solution.py:1074
  555.1 5.4 copy.87
  561.1 8.5 %pad_maximum_fusion.1.refs_2_ = bf16[4,2,2,2,192,768]{5,4,3,2,1,0:T(8,128)(2,1)} fusion(bf16[4,2,2,2,96,768]{5,4,3,2,1,0:T(8,128)(2,1)} %bitcast.234, bf16[4,2,2,2,96,768]{5,4,3,2,1,0:T(8,128)(2,1)} %bitcast.235), kind=kLoop, calls=%fused_computation.3 | loop fusion | flops 18874368 | bytes 18874368 | tf_op jit(solution)/shard_map/concatenate | solution.py:1090
  575.2 3.2 convolution_convert_fusion.4
  579.6 3.6 pad_maximum_fusion.4.refs_4_
  589.6 168.5 %reduce_weights.1 = (f32[192,768]{1,0:T(8,128)}, f32[96,768]{1,0:T(8,128)}, f32[192,768]{1,0:T(8,128)}, f32[96,768]{1,0:T(8,128)}, f32[32,1280]{1,0:T(8,128)}) custom-call(bf16[4,2,2,2,192,768]{5,4,3,2,1,0:T(8,128)(2,1)} %pad_maximum_fusion.refs_0_, bf16[4,2,2,2,96,768]{5,4,3,2,1,0:T(8,128)(2,1)} %pad_maximum_fusion.2.refs_1_, ...), custom_call_target="tpu_custom_call" | custom-call | tf_op jit(solution)/shard_map/reduce_weights/pallas_call | solution.py:738
  767.3 5.4 collective-permute-start.11
  776.5 9.2 %collective-permute-done.11 = f32[304,768]{1,0:T(8,128)S(1)} collective-permute-done((f32[304,768]{1,0:T(8,128)}, f32[304,768]{1,0:T(8,128)S(1)}, u32[]{:S(2)}, u32[]{:S(2)}) %collective-permute-start.11) | collective-permute-done | bytes 933920 | tf_op jit(solution)/shard_map/ppermute | solution.py:456
  (416 shorter events, 119.0 us)
Async XLA Ops:
  7.7 6.7 copy-start.18
  7.7 6.7 copy-start.20
  8.9 184.6 %collective-permute-start.1 = (s32[304]{0:T(512)S(1)}, s32[304]{0:T(512)S(1)}, u32[]{:S(2)}, u32[]{:S(2)}) collective-permute-start(s32[304]{0:T(512)S(1)} %get-tuple-element.153), channel_id=1, source_target_pairs={{0,2},{1,3},{2,0},{3,1},{4,6},{5,7},{6,4},{7,5},{8,10},{9,11},{10,... | collective-permute-start | bytes 3656 | tf_op jit(solution)/shard_map/ppermute | solution.py:456
  15.7 177.9 %collective-permute-start = (bf16[304,1536]{1,0:T(8,128)(2,1)S(1)}, bf16[304,1536]{1,0:T(8,128)(2,1)}, u32[]{:S(2)}, u32[]{:S(2)}) collective-permute-start(bf16[304,1536]{1,0:T(8,128)(2,1)S(1)} %get-tuple-element.130), channel_id=1, source_target_pairs={{0,2},{1,3},{2,0},{3,1},{4,6},{5,7},{6,4},{7,5},{8,10},{9,11},{10,... | collective-permute-start | bytes 2801672 | tf_op jit(solution)/shard_map/ppermute | solution.py:456
  180.9 20.4 %copy-start.8 = (bf16[32,1,24,768]{3,2,1,0:T(8,128)(2,1)}, bf16[32,1,24,768]{3,2,1,0:T(8,128)(2,1)S(1)}, u32[]{:S(2)}) copy-start(bf16[32,1,24,768]{3,2,1,0:T(8,128)(2,1)S(1)} %get-tuple-element.123) | copy-start | bytes 3538948
  184.9 12.7 %copy-start.54 = (f32[768]{0:T(1024)}, f32[768]{0:T(1024)S(1)}, u32[]{:S(2)}) copy-start(f32[768]{0:T(1024)S(1)} %get-tuple-element.99) | copy-start | bytes 9220
  184.9 63.2 %copy-start.60 = (f32[768]{0:T(1024)}, f32[768]{0:T(1024)S(1)}, u32[]{:S(2)}) copy-start(f32[768]{0:T(1024)S(1)} %get-tuple-element.93) | copy-start | bytes 9220
  184.9 8.4 %copy-start.25 = (bf16[4,2,2,2,32,1280]{5,4,3,2,1,0:T(8,128)(2,1)S(1)}, bf16[4,2,2,2,32,1280]{5,4,3,2,1,0:T(8,128)(2,1)}, u32[]{:S(2)}) copy-start(bf16[4,2,2,2,32,1280]{5,4,3,2,1,0:T(8,128)(2,1)} %get-tuple-element.42) | copy-start | bytes 7864324
  197.1 48.0 %copy-start = (f32[608,768]{1,0:T(8,128)}, f32[608,768]{1,0:T(8,128)S(1)}, u32[]{:S(2)}) copy-start(f32[608,768]{1,0:T(8,128)S(1)} %get-tuple-element.161) | copy-start | bytes 5603332
  200.9 25.1 %collective-permute-start.2 = (bf16[608,768]{1,0:T(8,128)(2,1)}, bf16[608,768]{1,0:T(8,128)(2,1)}, u32[]{:S(2)}, u32[]{:S(2)}) collective-permute-start(bf16[608,768]{1,0:T(8,128)(2,1)} %convolution_convert_fusion.17.ko_ref), channel_id=1, source_target_pairs={{0,1},{1,0},{2,3},{3,2},{4,5},{5,4},{6,7},{7,6},{8,9},{9,8},{10,11... | collective-permute-start | bytes 2801672 | tf_op jit(solution)/shard_map/ppermute | solution.py:460
  203.1 22.8 %collective-permute-start.3 = (bf16[608,768]{1,0:T(8,128)(2,1)}, bf16[608,768]{1,0:T(8,128)(2,1)}, u32[]{:S(2)}, u32[]{:S(2)}) collective-permute-start(bf16[608,768]{1,0:T(8,128)(2,1)} %add_convert_fusion.8.vo_ref), channel_id=1, source_target_pairs={{0,1},{1,0},{2,3},{3,2},{4,5},{5,4},{6,7},{7,6},{8,9},{9,8},{10,11... | collective-permute-start | bytes 2801672 | tf_op jit(solution)/shard_map/ppermute | solution.py:460
  204.7 9.6 %slice-start = ((s8[4718592]{0:T(1024)(128)(4,1)}), s8[4194304]{0:T(1024)(128)(4,1)S(1)}, s32[]{:S(2)}) async-start(s8[4718592]{0:T(1024)(128)(4,1)} %bitcast.231), calls=%async_computation | async-start | bytes 8388608
  247.7 8.9 %copy-start.2 = (f32[608,768]{1,0:T(8,128)}, f32[608,768]{1,0:T(8,128)S(1)}, u32[]{:S(2)}) copy-start(f32[608,768]{1,0:T(8,128)S(1)} %get-tuple-element.163) | copy-start | bytes 5603332
  247.7 8.9 %slice-start.4 = ((s8[4718592]{0:T(1024)(128)(4,1)}), s8[4194304]{0:T(1024)(128)(4,1)S(1)}, s32[]{:S(2)}) async-start(s8[4718592]{0:T(1024)(128)(4,1)} %bitcast.247), calls=%async_computation.4 | async-start | bytes 8388608
  248.1 8.6 %slice-start.5 = ((s8[4718592]{0:T(1024)(128)(4,1)}), s8[524288]{0:T(1024)(128)(4,1)S(1)}, s32[]{:S(2)}) async-start(s8[4718592]{0:T(1024)(128)(4,1)} %bitcast.247), calls=%async_computation.5 | async-start | bytes 1048576
  263.4 31.6 %collective-permute-start.4 = (bf16[608,768]{1,0:T(8,128)(2,1)}, bf16[608,768]{1,0:T(8,128)(2,1)}, u32[]{:S(2)}, u32[]{:S(2)}) collective-permute-start(bf16[608,768]{1,0:T(8,128)(2,1)} %convolution_convert_fusion.16.ko_ref), channel_id=1, source_target_pairs={{0,1},{1,0},{2,3},{3,2},{4,5},{5,4},{6,7},{7,6},{8,9},{9,8},{10,11... | collective-permute-start | bytes 2801672 | tf_op jit(solution)/shard_map/ppermute | solution.py:460
  265.7 29.4 %collective-permute-start.5 = (bf16[608,768]{1,0:T(8,128)(2,1)}, bf16[608,768]{1,0:T(8,128)(2,1)}, u32[]{:S(2)}, u32[]{:S(2)}) collective-permute-start(bf16[608,768]{1,0:T(8,128)(2,1)} %add_convert_fusion.5.vo_ref), channel_id=1, source_target_pairs={{0,1},{1,0},{2,3},{3,2},{4,5},{5,4},{6,7},{7,6},{8,9},{9,8},{10,11... | collective-permute-start | bytes 2801672 | tf_op jit(solution)/shard_map/ppermute | solution.py:460
  315.9 6.8 slice-start.10
  316.3 6.4 slice-start.11
  316.3 6.4 copy-start.17
  316.3 12.8 %slice-start.12 = ((s8[4718592]{0:T(1024)(128)(4,1)}), s8[4194304]{0:T(1024)(128)(4,1)S(1)}, s32[]{:S(2)}) async-start(s8[4718592]{0:T(1024)(128)(4,1)} %bitcast.261), calls=%async_computation.12 | async-start | bytes 8388608
  322.7 6.5 slice-start.13
  390.7 4.4 copy-start.39
  390.8 4.4 copy-start.45
  394.6 42.0 %collective-permute-start.7 = (bf16[608,768]{1,0:T(8,128)(2,1)}, bf16[608,768]{1,0:T(8,128)(2,1)}, u32[]{:S(2)}, u32[]{:S(2)}) collective-permute-start(bf16[608,768]{1,0:T(8,128)(2,1)} %get-tuple-element.53), channel_id=1, source_target_pairs={{0,1},{1,0},{2,3},{3,2},{4,5},{5,4},{6,7},{7,6},{8,9},{9,8},{10,11... | collective-permute-start | bytes 2801672 | tf_op jit(solution)/shard_map/ppermute | solution.py:460
  395.0 43.9 %collective-permute-start.8 = (bf16[608,768]{1,0:T(8,128)(2,1)}, bf16[608,768]{1,0:T(8,128)(2,1)}, u32[]{:S(2)}, u32[]{:S(2)}) collective-permute-start(bf16[608,768]{1,0:T(8,128)(2,1)} %get-tuple-element.55), channel_id=1, source_target_pairs={{0,1},{1,0},{2,3},{3,2},{4,5},{5,4},{6,7},{7,6},{8,9},{9,8},{10,11... | collective-permute-start | bytes 2801672 | tf_op jit(solution)/shard_map/ppermute | solution.py:460
  428.8 91.9 %collective-permute-start.6 = (f32[304,768]{1,0:T(8,128)}, f32[304,768]{1,0:T(8,128)}, u32[]{:S(2)}, u32[]{:S(2)}) collective-permute-start(f32[304,768]{1,0:T(8,128)} %get-tuple-element.129), channel_id=1, source_target_pairs={{0,2},{1,3},{2,0},{3,1},{4,6},{5,7},{6,4},{7,5},{8,10},{9,11},{10,... | collective-permute-start | bytes 2801672 | tf_op jit(solution)/shard_map/ppermute | solution.py:456
  429.7 6.9 copy-start.33
  429.7 6.9 copy-start.77
  441.8 6.3 slice-start.6
  441.8 6.3 slice-start.14
  442.5 5.6 slice-start.7
  442.5 5.6 slice-start.15
  442.5 11.6 %slice-start.2 = ((s8[4718592]{0:T(1024)(128)(4,1)}), s8[4194304]{0:T(1024)(128)(4,1)S(1)}, s32[]{:S(2)}) async-start(s8[4718592]{0:T(1024)(128)(4,1)} %bitcast.244), calls=%async_computation.2 | async-start | bytes 8388608
  448.2 6.0 copy-start.3
  448.2 6.0 slice-start.3
  464.9 36.4 %copy-start.29 = (bf16[32,1,24,768]{3,2,1,0:T(8,128)(2,1)S(1)}, bf16[32,1,24,768]{3,2,1,0:T(8,128)(2,1)}, u32[]{:S(2)}) copy-start(bf16[32,1,24,768]{3,2,1,0:T(8,128)(2,1)} %get-tuple-element.125) | copy-start | bytes 3538948
  504.8 64.8 %collective-permute-start.9 = (bf16[608,768]{1,0:T(8,128)(2,1)}, bf16[608,768]{1,0:T(8,128)(2,1)}, u32[]{:S(2)}, u32[]{:S(2)}) collective-permute-start(bf16[608,768]{1,0:T(8,128)(2,1)} %get-tuple-element.60), channel_id=1, source_target_pairs={{0,1},{1,0},{2,3},{3,2},{4,5},{5,4},{6,7},{7,6},{8,9},{9,8},{10,11... | collective-permute-start | bytes 2801672 | tf_op jit(solution)/shard_map/ppermute | solution.py:460
  504.9 67.0 %collective-permute-start.10 = (bf16[608,768]{1,0:T(8,128)(2,1)}, bf16[608,768]{1,0:T(8,128)(2,1)S(1)}, u32[]{:S(2)}, u32[]{:S(2)}) collective-permute-start(bf16[608,768]{1,0:T(8,128)(2,1)} %get-tuple-element.62), channel_id=1, source_target_pairs={{0,1},{1,0},{2,3},{3,2},{4,5},{5,4},{6,7},{7,6},{8,9},{9,8},{10,11... | collective-permute-start | bytes 2801672 | tf_op jit(solution)/shard_map/ppermute | solution.py:460
  514.1 6.5 copy-start.16
  514.1 6.5 copy-start.19
  514.1 6.6 copy-start.21
  555.1 5.9 copy-start.59
  561.0 8.5 %copy-start.27 = (bf16[32,1,24,768]{3,2,1,0:T(8,128)(2,1)S(1)}, bf16[32,1,24,768]{3,2,1,0:T(8,128)(2,1)}, u32[]{:S(2)}) copy-start(bf16[32,1,24,768]{3,2,1,0:T(8,128)(2,1)} %get-tuple-element.124) | copy-start | bytes 3538948
  561.0 8.5 %copy-start.75 = (bf16[608,768]{1,0:T(8,128)(2,1)S(1)}, bf16[608,768]{1,0:T(8,128)(2,1)}, u32[]{:S(2)}) copy-start(bf16[608,768]{1,0:T(8,128)(2,1)} %get-tuple-element.59) | copy-start | bytes 2801668
  561.1 10.9 %copy-start.23 = (f32[608,768]{1,0:T(8,128)S(1)}, f32[608,768]{1,0:T(8,128)}, u32[]{:S(2)}) copy-start(f32[608,768]{1,0:T(8,128)} %fusion.81) | copy-start | bytes 5603332
  767.3 8.6 %copy-start.52 = (f32[32,1280]{1,0:T(8,128)S(1)}, f32[32,1280]{1,0:T(8,128)}, u32[]{:S(2)}) copy-start(f32[32,1280]{1,0:T(8,128)} %get-tuple-element.63) | copy-start | bytes 491524
  767.3 18.4 %collective-permute-start.11 = (f32[304,768]{1,0:T(8,128)}, f32[304,768]{1,0:T(8,128)S(1)}, u32[]{:S(2)}, u32[]{:S(2)}) collective-permute-start(f32[304,768]{1,0:T(8,128)} %get-tuple-element.127), channel_id=1, source_target_pairs={{0,2},{1,3},{2,0},{3,1},{4,6},{5,7},{6,4},{7,5},{8,10},{9,11},{10,... | collective-permute-start | bytes 2801672 | tf_op jit(solution)/shard_map/ppermute | solution.py:456
  (63 other events, 144.8 us)

commit v2 on v0

--- a/solution.py
+++ b/solution.py
@@ -1,8 +1,11 @@
+import functools
 import math
 
 import jax
 import jax.numpy as jnp
 from jax import lax
+from jax.experimental import pallas as pl
+from jax.experimental.pallas import tpu as pltpu
 from jax.sharding import PartitionSpec as P
 
 HEAD_DIM = 64
@@ -411,9 +414,1490 @@
     )
 
 
+LOG2_E = 1.0 / math.log(2.0)
+LANES = 128
+BF16 = jnp.bfloat16
+F32 = jnp.float32
+MESH_ID = pl.DeviceIdType.MESH
+VMEM_LIMIT = 60 * 1024 * 1024
+
+
+def dot_nn(left, right):
+    return lax.dot_general(left, right, (((1,), (0,)), ((), ())), preferred_element_type=F32)
+
+
+def dot_nt(left, right):
+    return lax.dot_general(left, right, (((1,), (1,)), ((), ())), preferred_element_type=F32)
+
+
+def dot_tn(left, right):
+    return lax.dot_general(left, right, (((0,), (0,)), ((), ())), preferred_element_type=F32)
+
+
+def my_place():
+    gx = lax.axis_index("gx")
+    gy = lax.axis_index("gy")
+    return gx // 2, lax.rem(gx, 2), gy // 2, lax.rem(gy, 2)
+
+
+def device_at(z, x, y, core):
+    return (z * 2 + x, y * 2 + core)
+
+
+def flip_pairs(flip_y, flip_core):
+    pairs = []
+    for index in range(32):
+        gx, gy = divmod(index, 4)
+        pairs.append((index, gx * 4 + (gy ^ (2 * flip_y + flip_core))))
+    return pairs
+
+
+def to_partner(value):
+    return lax.ppermute(value, ("gx", "gy"), flip_pairs(1, 0))
+
+
+def to_sibling(value):
+    return lax.ppermute(value, ("gx", "gy"), flip_pairs(0, 1))
+
+
+class Copy:
+    def __init__(self, describe):
+        self.describe = describe
+
+    def start(self):
+        self.describe().start()
+
+    def wait(self):
+        self.describe().wait()
+
+    def wait_recv(self):
+        self.describe().wait_recv()
+
+    def wait_send(self):
+        self.describe().wait_send()
+
+
+def remote(src, dst, send_sem, recv_sem, device):
+    return Copy(
+        lambda: pltpu.make_async_remote_copy(
+            src_ref=src,
+            dst_ref=dst,
+            send_sem=send_sem,
+            recv_sem=recv_sem,
+            device_id=device,
+            device_id_type=MESH_ID,
+        )
+    )
+
+
+def local_copy(src, dst, sem):
+    return Copy(lambda: pltpu.make_async_copy(src, dst, sem))
+
+
+def block_at(ref, order, z, x, y, *rest):
+    place = (z, x, y) if order == "zxy" else (y, z, x)
+    return ref.at[(*place, *rest)]
+
+
+def full_at(ref, order, z, x, y, core, *rest):
+    place = (z, x, y, core) if order == "zxy" else (y, core, z, x)
+    return ref.at[(*place, *rest)]
+
+
+def added(left, right):
+    return (left.astype(F32) + right.astype(F32)).astype(BF16)
+
+
+def hbm():
+    return pl.BlockSpec(memory_space=pl.ANY)
+
+
+def vmem():
+    return pl.BlockSpec(memory_space=pltpu.VMEM)
+
+
+def dma_sems(count):
+    return pltpu.SemaphoreType.DMA((count,))
+
+
+class GatherZ:
+    space = out_space = pltpu.VMEM
+
+    def __init__(self, shard):
+        self.rows, self.columns = shard.shape
+        self.outs = [((4, self.rows, self.columns), BF16)]
+        self.scratch = [dma_sems(3), dma_sems(3), dma_sems(1)]
+
+    def copies(self, place, refs):
+        shard, out, send, recv, local = refs
+        z, x, y, core = place
+        keep = local_copy(shard, out.at[z], local.at[0])
+        return keep, [
+            remote(
+                shard, out.at[z], send.at[k], recv.at[k], device_at(lax.rem(z + k + 1, 4), x, y, core)
+            )
+            for k in range(3)
+        ]
+
+    def step(self, number, place, refs):
+        keep, copies = self.copies(place, refs)
+        if number == 0:
+            keep.start()
+            for copy in copies:
+                copy.start()
+        else:
+            keep.wait()
+            for copy in copies:
+                copy.wait()
+
+
+class GatherXY:
+    space, out_space = pltpu.VMEM, pl.ANY
+
+    def __init__(self, column, order):
+        unused, self.rows, self.columns = column.shape
+        self.order = order
+        shape = (4, 2, 2, 2) if order == "zxy" else (2, 2, 4, 2)
+        self.outs = [((*shape, self.rows, self.columns), BF16)]
+        self.scratch = [dma_sems(5), dma_sems(5), dma_sems(1)]
+
+    def copies(self, place, refs):
+        column, full, send, recv, local = refs
+        z, x, y, core = place
+        half = self.rows // 2
+        low, high = pl.ds(0, half), pl.ds(half, half)
+        every = slice(None)
+
+        def at(*where):
+            return full_at(full, self.order, *where)
+
+        def copy(slot, src, dst, device):
+            return remote(src, dst, send.at[slot], recv.at[slot], device)
+
+        to_x, to_y = device_at(z, 1 - x, y, core), device_at(z, x, 1 - y, core)
+        here = at(every, x, y, core)
+        keep = local_copy(column, here, local.at[0])
+        first = [
+            copy(0, column.at[:, low], at(every, x, y, core, low), to_x),
+            copy(1, column.at[:, high], at(every, x, y, core, high), to_y),
+        ]
+        two_low, two_high = at(every, every, y, core, low), at(every, x, every, core, high)
+        second = [copy(2, two_low, two_low, to_y), copy(3, two_high, two_high, to_x)]
+        all_here = at(every, every, every, core)
+        third = [copy(4, all_here, all_here, device_at(z, x, y, 1 - core))]
+        return keep, first, second, third
+
+    def step(self, number, place, refs):
+        keep, first, second, third = self.copies(place, refs)
+        if number == 0:
+            keep.start()
+            for copy in first:
+                copy.start()
+        elif number == 1:
+            keep.wait()
+            for copy in first:
+                copy.wait_recv()
+            for copy in second:
+                copy.start()
+        elif number == 2:
+            for copy in second:
+                copy.wait_recv()
+            for copy in third:
+                copy.start()
+        else:
+            for copy in third:
+                copy.wait_recv()
+            for copy in first + second + third:
+                copy.wait_send()
+
+
+class SumCore:
+    space = out_space = pltpu.VMEM
+
+    def __init__(self, part):
+        self.rows, self.columns = part.shape[-2:]
+        shape = (4, 2, 2, self.rows, self.columns)
+        self.outs = [(shape, BF16)]
+        self.scratch = [pltpu.VMEM(shape, BF16), dma_sems(1), dma_sems(1)]
+
+    def step(self, number, place, refs):
+        part, out, arrived, send, recv = refs
+        z, x, y, core = place
+        copy = remote(
+            part.at[:, :, :, 1 - core], arrived, send.at[0], recv.at[0], device_at(z, x, y, 1 - core)
+        )
+        if number == 0:
+            copy.start()
+        else:
+            copy.wait()
+
+            def add_one(i, carry):
+                a, b, c = i // 4, lax.rem(i // 2, 2), lax.rem(i, 2)
+                out[a, b, c] = added(part[a, b, c, core], arrived[a, b, c])
+                return carry
+
+            lax.fori_loop(0, 16, add_one, 0)
+
+
+class SumXY:
+    space = out_space = pltpu.VMEM
+
+    def __init__(self, part, order):
+        self.rows, self.columns = part.shape[-2:]
+        self.order = order
+        half = self.rows // 2
+        by_x = (4, 2, half, self.columns)
+        by_y = by_x if order == "zxy" else (2, 4, half, self.columns)
+        self.outs = [((4, self.rows, self.columns), BF16)]
+        self.scratch = [
+            pltpu.VMEM(by_x, BF16),
+            pltpu.VMEM(by_y, BF16),
+            pltpu.VMEM(by_x, BF16),
+            pltpu.VMEM(by_y, BF16),
+            pltpu.VMEM((2, 4, half, self.columns), BF16),
+            dma_sems(4),
+            dma_sems(4),
+        ]
+
+    def step(self, number, place, refs):
+        part, out, in_a, in_b, sum_a, sum_b, third, send, recv = refs
+        z, x, y, core = place
+        half = self.rows // 2
+        low, high = pl.ds(0, half), pl.ds(half, half)
+        every = slice(None)
+        to_x, to_y = device_at(z, 1 - x, y, core), device_at(z, x, 1 - y, core)
+
+        def at(*where):
+            return block_at(part, self.order, *where)
+
+        def by_y(ref, a, b):
+            return ref.at[a, b] if self.order == "zxy" else ref.at[b, a]
+
+        def copy(slot, src, dst, device):
+            return remote(src, dst, send.at[slot], recv.at[slot], device)
+
+        first = [
+            copy(0, at(every, every, 1 - y, low), in_a, to_y),
+            copy(1, at(every, 1 - x, every, high), in_b, to_x),
+        ]
+        second = [
+            copy(2, sum_a.at[:, 1 - x], third.at[0], to_x),
+            copy(3, by_y(sum_b, every, 1 - y), third.at[1], to_y),
+        ]
+        if number == 0:
+            for one in first:
+                one.start()
+        elif number == 1:
+            for one in first:
+                one.wait_recv()
+
+            def add_one(i, carry):
+                a, b = i // 2, lax.rem(i, 2)
+                sum_a[a, b] = added(at(a, b, y, low)[...], in_a[a, b])
+                by_y(sum_b, a, b)[...] = added(at(a, x, b, high)[...], by_y(in_b, a, b)[...])
+                return carry
+
+            lax.fori_loop(0, 8, add_one, 0)
+            for one in second:
+                one.start()
+        else:
+            for one in second:
+                one.wait_recv()
+
+            def add_two(a, carry):
+                out[a, low] = added(sum_a[a, x], third[0, a])
+                out[a, high] = added(by_y(sum_b, a, y)[...], third[1, a])
+                return carry
+
+            lax.fori_loop(0, 4, add_two, 0)
+            for one in first + second:
+                one.wait_send()
+
+
+class SumZ:
+    space = out_space = pltpu.VMEM
+
+    def __init__(self, part):
+        unused, self.rows, self.columns = part.shape
+        self.outs = [((self.rows, self.columns), F32)]
+        self.scratch = [pltpu.VMEM((3, self.rows, self.columns), BF16), dma_sems(3), dma_sems(3)]
+
+    def step(self, number, place, refs):
+        part, out, arrived, send, recv = refs
+        z, x, y, core = place
+        copies = []
+        for k in range(3):
+            to_z = lax.rem(z + k + 1, 4)
+            copies.append(
+                remote(
+                    part.at[to_z], arrived.at[k], send.at[k], recv.at[k], device_at(to_z, x, y, core)
+                )
+            )
+        if number == 0:
+            for copy in copies:
+                copy.start()
+        else:
+            for copy in copies:
+                copy.wait()
+            total = part[z].astype(F32)
+            for k in range(3):
+                total = total + arrived[k].astype(F32)
+            out[...] = total
+
+
+class Carried:
+    def __init__(self, *entries):
+        self.stages = [entry[0] for entry in entries]
+        self.links = [entry[1] if isinstance(entry[1], int) else None for entry in entries]
+        self.arrays = [entry[1] for entry in entries if not isinstance(entry[1], int)]
+        self.events = [entry[2] for entry in entries]
+        self.in_specs = [
+            pl.BlockSpec(memory_space=stage.space)
+            for stage, link in zip(self.stages, self.links)
+            if link is None
+        ]
+        self.out_shape = [jax.ShapeDtypeStruct(*out) for stage in self.stages for out in stage.outs]
+        self.out_specs = [pl.BlockSpec(memory_space=stage.out_space) for stage in self.stages]
+        self.scratch = [item for stage in self.stages for item in stage.scratch]
+
+    def run(self, event, place, ins, outs, scratch):
+        at, taken = 0, 0
+        for index, stage in enumerate(self.stages):
+            size = len(stage.scratch)
+            if self.links[index] is None:
+                source = ins[taken]
+                taken += 1
+            else:
+                source = outs[self.links[index]]
+            refs = (source, outs[index], *scratch[at : at + size])
+            at += size
+            for number, when in enumerate(self.events[index]):
+                if when == event:
+                    stage.step(number, place, refs)
+
+    def first(self):
+        return min((when for events in self.events for when in events), default=None)
+
+
+def greet_signal(place):
+    z, x, y, core = place
+    barrier = pltpu.get_barrier_semaphore()
+    others = [device_at(lax.rem(z + k, 4), x, y, core) for k in (1, 2, 3)]
+    others += [device_at(z, 1 - x, y, core), device_at(z, x, 1 - y, core)]
+    others += [device_at(z, x, y, 1 - core)]
+    for other in others:
+        pl.semaphore_signal(barrier, inc=1, device_id=other, device_id_type=MESH_ID)
+
+
+def greet_wait():
+    pl.semaphore_wait(pltpu.get_barrier_semaphore(), 6)
+
+
+def comm_kernel(steps, count, ins, *refs):
+    total = len(ins)
+    named = [entry for entry in ins if not isinstance(entry, int)]
+    in_refs = list(refs[: len(named)])
+    out_refs = refs[len(named) : len(named) + total]
+    scratch = refs[len(named) + total :]
+    place = my_place()
+    greet_signal(place)
+    greet_wait()
+    bound, at, taken = [], 0, 0
+    for index, stage in enumerate(count):
+        if isinstance(ins[index], int):
+            source = out_refs[ins[index]]
+        else:
+            source = in_refs[taken]
+            taken += 1
+        size = len(stage.scratch)
+        bound.append((source, out_refs[index], *scratch[at : at + size]))
+        at += size
+    for index, number in steps:
+        count[index].step(number, place, bound[index])
+
+
+def run_stages(stages, ins, steps, collective_id, name):
+    named = [entry for entry in ins if not isinstance(entry, int)]
+    specs = [
+        pl.BlockSpec(memory_space=stage.space)
+        for stage, entry in zip(stages, ins)
+        if not isinstance(entry, int)
+    ]
+    marks = tuple(entry if isinstance(entry, int) else None for entry in ins)
+    return pl.pallas_call(
+        functools.partial(comm_kernel, steps, stages, marks),
+        out_shape=[jax.ShapeDtypeStruct(*stage.outs[0]) for stage in stages],
+        in_specs=specs,
+        out_specs=[pl.BlockSpec(memory_space=stage.out_space) for stage in stages],
+        scratch_shapes=[item for stage in stages for item in stage.scratch],
+        compiler_params=pltpu.CompilerParams(
+            collective_id=collective_id, has_side_effects=True, vmem_limit_bytes=VMEM_LIMIT
+        ),
+        name=name,
+    )(*named)
+
+
+def carrying(
+    body, carried, steps, collective_id, name, in_specs, out_specs, out_shape, scratch, flops, args,
+    own_greet=False,
+):
+    n_in, n_out, n_scratch = len(in_specs), len(out_specs), len(scratch)
+    carry_in, carry_out = len(carried.in_specs), len(carried.out_specs)
+    greets = -1 if own_greet else carried.first()
+
+    def kernel(*refs):
+        ins, refs = refs[:n_in], refs[n_in:]
+        c_ins, refs = refs[:carry_in], refs[carry_in:]
+        outs, refs = refs[:n_out], refs[n_out:]
+        c_outs, refs = refs[:carry_out], refs[carry_out:]
+        own, c_scratch = refs[:n_scratch], refs[n_scratch:]
+        step = pl.program_id(0)
+        place = my_place()
+
+        def event(number):
+            if greets is not None and number == greets:
+                greet_wait()
+            carried.run(number, place, c_ins, c_outs, c_scratch)
+
+        if greets is not None:
+            pl.when(step == 0)(lambda: greet_signal(place))
+        numbers = sorted({when for events in carried.events for when in events})
+        if 0 in numbers:
+            pl.when(step == 0)(functools.partial(event, 0))
+        body(step, place, *ins, *outs, *own)
+        for number in numbers:
+            if number > 0:
+                pl.when(step == number - 1)(functools.partial(event, number))
+
+    params = {"vmem_limit_bytes": VMEM_LIMIT}
+    if greets is not None:
+        params.update(collective_id=collective_id, has_side_effects=True)
+    results = pl.pallas_call(
+        kernel,
+        grid=(steps,),
+        out_shape=[*out_shape, *carried.out_shape],
+        in_specs=[*in_specs, *carried.in_specs],
+        out_specs=[*out_specs, *carried.out_specs],
+        scratch_shapes=[*scratch, *carried.scratch],
+        compiler_params=pltpu.CompilerParams(**params),
+        cost_estimate=pl.CostEstimate(flops=flops, bytes_accessed=flops // 300, transcendentals=0),
+        name=name,
+    )(*args, *carried.arrays)
+    return results[:n_out], results[n_out:]
+
+
+def lane_marks(head):
+    lane = lax.broadcasted_iota(jnp.int32, (1, LANES), 1)
+    own = (lane // HEAD_DIM == head).astype(F32)
+    spare = HEAD_DIM * (1 - head)
+    return lane, own, spare
+
+
+def split_three(column):
+    high = column.astype(BF16).astype(F32)
+    rest = column - high
+    middle = rest.astype(BF16).astype(F32)
+    return high, middle, rest - middle
+
+
+def attention_body(block, pair, place, q_ref, ko_ref, ks_ref, vo_ref, vs_ref, bias_ref, out_ref, exact_ref, lse_ref, keys, values):
+    rows = q_ref.shape[0]
+    values[0:rows] = vo_ref[...]
+    values[rows:] = vs_ref[...]
+    lanes = lax.broadcasted_iota(jnp.int32, (1, LANES), 1)
+
+    @pl.when(pair == 0)
+    def _():
+        lse_ref[...] = jnp.zeros_like(lse_ref)
+
+    mixed = [[], []]
+    totals = [[], []]
+    for head in range(2):
+        lane, own, spare = lane_marks(head)
+        own16 = own.astype(BF16)
+        at_spare = (lane == spare).astype(BF16)
+        keys[0:rows] = ko_ref[...] * own16 + bias_ref[0:rows] * at_spare
+        keys[rows:] = ks_ref[...] * own16 + bias_ref[rows:] * at_spare
+        for start in range(0, rows, block):
+            query = q_ref[start : start + block] * own16 + at_spare
+            scores = dot_nt(query, keys[...])
+            top = jnp.max(scores, axis=-1, keepdims=True)
+            weights = jnp.exp2(scores - top)
+            total = jnp.sum(weights, axis=-1, keepdims=True)
+            summed = dot_nn(weights.astype(BF16), values[...])
+            mixed[head].append(summed * (1.0 / total))
+            totals[head].append(top + jnp.log2(total))
+    for index, start in enumerate(range(0, rows, block)):
+        rows_at = slice(start, start + block)
+        both = jnp.where(lanes < HEAD_DIM, mixed[0][index], mixed[1][index])
+        out_ref[rows_at] = both.astype(BF16)
+        exact_ref[rows_at] = both
+        held = lse_ref[rows_at]
+        held = jnp.where(lanes == 2 * pair, totals[0][index], held)
+        lse_ref[rows_at] = jnp.where(lanes == 2 * pair + 1, totals[1][index], held)
+
+
+def attention_forward(queries, keys_own, keys_sib, values_own, values_sib, bias, carried, collective_id):
+    rows, width = queries.shape
+    column = pl.BlockSpec((rows, LANES), lambda pair: (0, pair))
+    return carrying(
+        functools.partial(attention_body, rows // 2),
+        carried,
+        width // LANES,
+        collective_id,
+        "attention_forward",
+        [column] * 5 + [pl.BlockSpec((2 * rows, LANES), lambda pair: (0, 0))],
+        [column, column, pl.BlockSpec((rows, LANES), lambda pair: (0, 0))],
+        [
+            jax.ShapeDtypeStruct((rows, width), BF16),
+            jax.ShapeDtypeStruct((rows, width), F32),
+            jax.ShapeDtypeStruct((rows, LANES), F32),
+        ],
+        [pltpu.VMEM((2 * rows, LANES), BF16), pltpu.VMEM((2 * rows, LANES), BF16)],
+        8 * rows * 2 * rows * width,
+        (queries, keys_own, keys_sib, values_own, values_sib, bias),
+    )
+
+
+def attention_back_body(
+    pair, place, q_ref, ko_ref, ks_ref, vo_ref, vs_ref, do_ref, mix_ref, lse_ref, bias_ref,
+    dq_ref, dko_ref, dks_ref, dvo_ref, dvs_ref,
+):
+    rows = q_ref.shape[0]
+    block = rows // 2
+    lanes = lax.broadcasted_iota(jnp.int32, (1, LANES), 1)
+    query = q_ref[...]
+    grad = do_ref[...]
+    product = grad.astype(F32) * mix_ref[...]
+    heads = []
+    for head in range(2):
+        lane, own, spare = lane_marks(head)
+        own16 = own.astype(BF16)
+        lse = jnp.sum(jnp.where(lanes == 2 * pair + head, lse_ref[...], 0.0), axis=-1, keepdims=True)
+        inner = jnp.sum(product * own, axis=-1, keepdims=True)
+        lse_parts, inner_parts = split_three(-lse), split_three(-inner)
+        query_own = query * own16
+        grad_own = grad * own16
+        query_aug = jnp.where(lane == spare, 1.0, 0.0)
+        grad_aug = jnp.zeros((1, LANES), F32)
+        for k in range(3):
+            query_aug = jnp.where(lane == spare + 1 + k, lse_parts[k], query_aug)
+            grad_aug = jnp.where(lane == spare + 1 + k, inner_parts[k], grad_aug)
+        query_aug = query_own + query_aug.astype(BF16)
+        grad_aug = grad_own + grad_aug.astype(BF16)
+        at_spare = (lane == spare).astype(BF16)
+        ones = ((lane > spare) & (lane < spare + 4)).astype(BF16)
+        heads.append((own16, at_spare, ones, query_own, grad_own, query_aug, grad_aug))
+    query_grad = jnp.zeros((LANES, rows), F32)
+    for side, (k_ref, v_ref, dk_ref, dv_ref) in enumerate(
+        ((ko_ref, vo_ref, dko_ref, dvo_ref), (ks_ref, vs_ref, dks_ref, dvs_ref))
+    ):
+        for start in range(0, rows, block):
+            at = slice(start, start + block)
+            key, value = k_ref[at], v_ref[at]
+            shift = bias_ref[side * rows + start : side * rows + start + block]
+            key_grad = jnp.zeros((block, LANES), F32)
+            value_grad = jnp.zeros((block, LANES), F32)
+            for own16, at_spare, ones, query_own, grad_own, query_aug, grad_aug in heads:
+                key_own = key * own16
+                weights = jnp.exp2(dot_nt(key_own + shift * at_spare + ones, query_aug))
+                weight_grad = dot_nt(value * own16 + ones, grad_aug)
+                score_grad = (weights * weight_grad).astype(BF16)
+                value_grad = value_grad + dot_nn(weights.astype(BF16), grad_own)
+                key_grad = key_grad + dot_nn(score_grad, query_own)
+                query_grad = query_grad + dot_tn(key_own, score_grad)
+            dk_ref[at] = (key_grad * (1.0 / LOG2_E)).astype(BF16)
+            dv_ref[at] = value_grad.astype(BF16)
+    dq_ref[...] = (jnp.transpose(query_grad) * HEAD_DIM ** (-0.5)).astype(BF16)
+
+
+def attention_backward(
+    queries, keys_own, keys_sib, values_own, values_sib, mixed_grad, mixed, lse, bias, carried, collective_id
+):
+    rows, width = queries.shape
+    column = pl.BlockSpec((rows, LANES), lambda pair: (0, pair))
+    fixed = pl.BlockSpec((rows, LANES), lambda pair: (0, 0))
+    return carrying(
+        attention_back_body,
+        carried,
+        width // LANES,
+        collective_id,
+        "attention_backward",
+        [column] * 7 + [fixed, pl.BlockSpec((2 * rows, LANES), lambda pair: (0, 0))],
+        [column] * 5,
+        [jax.ShapeDtypeStruct((rows, width), BF16)] * 5,
+        [],
+        20 * rows * 2 * rows * width,
+        (queries, keys_own, keys_sib, values_own, values_sib, mixed_grad, mixed, lse, bias),
+    )
+
+
+def norm_parts(values):
+    row_mean = jnp.mean(values, axis=-1, keepdims=True)
+    centred = values - row_mean
+    row_var = jnp.mean(centred * centred, axis=-1, keepdims=True)
+    rstd = lax.rsqrt(row_var + EPSILON)
+    return centred * rstd, rstd
+
+
+def norm_back(values, gain, grad):
+    normed, rstd = norm_parts(values)
+    scaled = grad * gain
+    first = jnp.mean(scaled, axis=-1, keepdims=True)
+    second = jnp.mean(scaled * normed, axis=-1, keepdims=True)
+    back = (scaled - first - normed * second) * rstd
+    return back, jnp.sum(grad * normed, axis=0, keepdims=True), jnp.sum(grad, axis=0, keepdims=True)
+
+
+def feed_forward_body(
+    step, place, mid_ref, gain_ref, shift_ref, up_bias_ref, down_bias_ref, weight_ref,
+    out_ref, hidden_ref, slope_ref, act_ref, total_ref,
+):
+    rows, features = mid_ref.shape
+    half = rows // 2
+    up_rows = weight_ref.shape[4] // 2
+    halves = [slice(0, half), slice(half, rows)]
+
+    @pl.when(step == 0)
+    def _():
+        for at in halves:
+            values = mid_ref[at]
+            normed, unused = norm_parts(values)
+            act_ref[at] = (normed * gain_ref[...] + shift_ref[...]).astype(BF16)
+            total_ref[at] = values + down_bias_ref[...]
+
+    weight_up = weight_ref[0, 0, :, :, 0:up_rows, :].reshape(features, features)
+    weight_down = weight_ref[0, 0, :, :, up_rows:, :].reshape(features, features)
+    for at in halves:
+        pre_act = dot_nn(act_ref[at], weight_up) + up_bias_ref[0]
+        below = 0.5 * (1.0 + lax.erf(pre_act * SQRT_HALF))
+        hidden = (pre_act * below).astype(BF16)
+        hidden_ref[at] = hidden
+        slope = below + pre_act * jnp.exp(-0.5 * pre_act * pre_act) * NORMAL_PEAK
+        slope_ref[at] = slope.astype(BF16)
+        total_ref[at] += dot_nt(hidden, weight_down)
+
+    @pl.when(step == pl.num_programs(0) - 1)
+    def _():
+        out_ref[...] = total_ref[...]
+
+
+def whole(shape):
+    return pl.BlockSpec(shape, lambda step: (0,) * len(shape), pipeline_mode=pl.Buffered(1))
+
+
+def feed_forward(middle, gain, shift, up_bias, down_bias, weights, carried, collective_id):
+    rows, features = middle.shape
+    blocks = weights.shape[0] * weights.shape[1]
+    column = pl.BlockSpec((rows, features), lambda step: (0, step))
+    line = whole((1, features))
+    return carrying(
+        feed_forward_body,
+        carried,
+        blocks,
+        collective_id,
+        "feed_forward",
+        [
+            whole((rows, features)),
+            line,
+            line,
+            pl.BlockSpec((1, 1, features), lambda step: (step, 0, 0)),
+            line,
+            pl.BlockSpec((1, 1) + weights.shape[2:], lambda step: (step // 2, lax.rem(step, 2), 0, 0, 0, 0)),
+        ],
+        [whole((rows, features)), column, column],
+        [
+            jax.ShapeDtypeStruct((rows, features), F32),
+            jax.ShapeDtypeStruct((rows, blocks * features), BF16),
+            jax.ShapeDtypeStruct((rows, blocks * features), BF16),
+        ],
+        [pltpu.VMEM((rows, features), BF16), pltpu.VMEM((rows, features), F32)],
+        4 * rows * features * features * blocks,
+        (middle, gain, shift, up_bias, down_bias, weights),
+    )
+
+
+def feed_forward_back_body(
+    step, place, grad_ref, mid_ref, gain_ref, shift_ref, hidden_ref, slope_ref, weight_ref,
+    out_ref, line_ref, up_bias_ref, part_ref,
+    grad16_ref, act_t_ref, grad_t_ref, pre_grad_ref, total_ref, sent_ref, arrived_ref, send, recv,
+):
+    z, x, y, core = place
+    rows, features = mid_ref.shape
+    half = rows // 2
+    up_rows = weight_ref.shape[4] // 2
+    halves = [slice(0, half), slice(half, rows)]
+    to_core = device_at(z, x, y, 1 - core)
+
+    def to_sibling_core(block):
+        return remote(sent_ref.at[block], arrived_ref.at[block], send.at[block], recv.at[block], to_core)
+
+    @pl.when(step == 0)
+    def _():
+        normed, unused = norm_parts(mid_ref[...])
+        act_t_ref[...] = jnp.transpose(normed * gain_ref[...] + shift_ref[...]).astype(BF16)
+        grad16_ref[...] = grad_ref[...].astype(BF16)
+        grad_t_ref[...] = jnp.transpose(grad_ref[...]).astype(BF16)
+        total_ref[...] = jnp.zeros_like(total_ref)
+
+    weight_up = weight_ref[0, 0, :, :, 0:up_rows, :].reshape(features, features)
+    weight_down = weight_ref[0, 0, :, :, up_rows:, :].reshape(features, features)
+    lines = jnp.zeros((1, features), F32)
+    for at in halves:
+        hidden_grad = dot_nn(grad16_ref[at], weight_down)
+        pre_grad = (hidden_grad * slope_ref[0, at].astype(F32)).astype(BF16)
+        pre_grad_ref[at] = pre_grad
+        lines = lines + jnp.sum(pre_grad.astype(F32), axis=0, keepdims=True)
+        total_ref[at] += dot_nt(pre_grad, weight_up)
+    up_bias_ref[0] = lines
+
+    def parts(store):
+        deep = 2 * up_rows
+        for a in range(4):
+            at = slice(a * deep, (a + 1) * deep)
+            store(a, slice(0, up_rows), dot_nn(act_t_ref[at], pre_grad_ref[...]))
+            store(a, slice(up_rows, deep), dot_nn(grad_t_ref[at], hidden_ref[0]))
+
+    @pl.when(step < 2)
+    def _():
+        def store(a, at, value):
+            sent_ref[step, a, :, at, :] = value.reshape(2, up_rows, features).astype(BF16)
+
+        parts(store)
+        pl.when(step == 0)(greet_wait)
+        to_sibling_core(step).start()
+
+    @pl.when(step >= 2)
+    def _():
+        block = step - 2
+        to_sibling_core(block).wait_recv()
+
+        def store(a, at, value):
+            other = arrived_ref[block, a, :, at, :].astype(F32)
+            part_ref[block, a, :, at, :] = (value.reshape(2, up_rows, features) + other).astype(BF16)
+
+        parts(store)
+
+    @pl.when(step == 3)
+    def _():
+        gain_sum = jnp.zeros((1, features), F32)
+        shift_sum = jnp.zeros((1, features), F32)
+        down_sum = jnp.zeros((1, features), F32)
+        for at in halves:
+            back, gain_part, shift_part = norm_back(mid_ref[at], gain_ref[...], total_ref[at])
+            out_ref[at] = grad_ref[at] + back
+            gain_sum, shift_sum = gain_sum + gain_part, shift_sum + shift_part
+            down_sum = down_sum + jnp.sum(grad16_ref[at].astype(F32), axis=0, keepdims=True)
+        line_ref[0:1] = gain_sum
+        line_ref[1:2] = shift_sum
+        line_ref[2:3] = down_sum
+        for block in range(2):
+            to_sibling_core(block).wait_send()
+
+
+def feed_forward_backward(grad, middle, gain, shift, hidden, slope, weights, carried, collective_id):
+    rows, features = middle.shape
+    blocks = weights.shape[0] * weights.shape[1]
+    deep = weights.shape[4]
+    line = whole((1, features))
+
+    def block_of(step):
+        core = lax.rem(lax.axis_index("gy"), 2)
+        return lax.rem(step, 2), jnp.where(step < 2, 1 - core, core)
+
+    def column_of(step):
+        y, core = block_of(step)
+        return 0, y * 2 + core
+
+    def weight_of(step):
+        y, core = block_of(step)
+        return y, core, 0, 0, 0, 0
+
+    column = pl.BlockSpec((1, rows, features), lambda step: (column_of(step)[1], 0, 0))
+    pair = (2, 4, 2, deep, features)
+    return carrying(
+        feed_forward_back_body,
+        carried,
+        blocks,
+        collective_id,
+        "feed_forward_backward",
+        [
+            whole((rows, features)),
+            whole((rows, features)),
+            line,
+            line,
+            column,
+            column,
+            pl.BlockSpec((1, 1) + weights.shape[2:], weight_of),
+        ],
+        [
+            whole((rows, features)),
+            whole((8, features)),
+            pl.BlockSpec((1, 1, features), lambda step: (column_of(step)[1], 0, 0)),
+            whole(pair),
+        ],
+        [
+            jax.ShapeDtypeStruct((rows, features), F32),
+            jax.ShapeDtypeStruct((8, features), F32),
+            jax.ShapeDtypeStruct((blocks, 1, features), F32),
+            jax.ShapeDtypeStruct(pair, BF16),
+        ],
+        [
+            pltpu.VMEM((rows, features), BF16),
+            pltpu.VMEM((features, rows), BF16),
+            pltpu.VMEM((features, rows), BF16),
+            pltpu.VMEM((rows, features), BF16),
+            pltpu.VMEM((rows, features), F32),
+            pltpu.VMEM(pair, BF16),
+            pltpu.VMEM(pair, BF16),
+            dma_sems(2),
+            dma_sems(2),
+        ],
+        8 * rows * features * features * blocks,
+        (grad, middle, gain, shift, hidden, slope, weights),
+        own_greet=True,
+    )
+
+
+class Gather:
+    def __init__(self, place, shard, full, order, start, rows, send, recv, local):
+        z, x, y, core = place
+        half = rows // 2
+        every = slice(None)
+        both, low, high = pl.ds(start, rows), pl.ds(start, half), pl.ds(start + half, half)
+
+        def at(*where):
+            return full_at(full, order, *where)
+
+        def copy(slot, src, dst, device):
+            return remote(src, dst, send.at[slot], recv.at[slot], device)
+
+        def same(slot, ref, device):
+            return copy(slot, ref, ref, device)
+
+        to_x, to_y = device_at(z, 1 - x, y, core), device_at(z, x, 1 - y, core)
+        own = at(z, x, y, core, both)
+        self.keep = local_copy(shard.at[both], own, local)
+        self.along_z = [
+            copy(k, shard.at[both], own, device_at(lax.rem(z + k + 1, 4), x, y, core)) for k in range(3)
+        ]
+        self.first = [
+            same(3, at(every, x, y, core, low), to_x),
+            same(4, at(every, x, y, core, high), to_y),
+        ]
+        self.second = [
+            same(5, at(every, every, y, core, low), to_y),
+            same(6, at(every, x, every, core, high), to_x),
+        ]
+        self.third = [same(7, at(every, every, every, core, both), device_at(z, x, y, 1 - core))]
+
+    def start_z(self):
+        self.keep.start()
+        for copy in self.along_z:
+            copy.start()
+
+    def start_first(self):
+        self.keep.wait()
+        for copy in self.along_z:
+            copy.wait_recv()
+        for copy in self.first:
+            copy.start()
+
+    def start_second(self):
+        for copy in self.first:
+            copy.wait_recv()
+        for copy in self.second:
+            copy.start()
+
+    def start_third(self):
+        for copy in self.second:
+            copy.wait_recv()
+        for copy in self.third:
+            copy.start()
+
+    def finish(self):
+        for copy in self.third:
+            copy.wait_recv()
+
+    def drain(self):
+        for copy in self.along_z + self.first + self.second + self.third:
+            copy.wait_send()
+
+
+class GatherChain:
+    def __init__(self, gathers):
+        self.gathers = gathers
+
+    def begin(self):
+        for gather in self.gathers[:2]:
+            gather.start_z()
+
+    def follow(self):
+        for index in range(2):
+            self.gathers[index].start_first()
+            self.gathers[index + 2].start_z()
+        self.gathers[0].start_second()
+
+    def turn(self, index):
+        count = len(self.gathers)
+        self.gathers[index].start_third()
+        if index + 1 < count:
+            self.gathers[index + 1].start_second()
+        if index + 2 < count:
+            self.gathers[index + 2].start_first()
+        if index + 4 < count:
+            self.gathers[index + 4].start_z()
+
+    def finish(self, index):
+        self.gathers[index].finish()
+
+    def drain(self):
+        for gather in self.gathers:
+            gather.drain()
+
+
+def spread_matrix(width, columns):
+    row = lax.broadcasted_iota(jnp.int32, (LANES, columns), 0)
+    lane = lax.broadcasted_iota(jnp.int32, (LANES, columns), 1)
+    return (row == lax.rem(lane, width)).astype(F32).astype(BF16)
+
+
+def forward_kernel(sizes, *refs):
+    layers, count, owned, up_rows = sizes
+    (choose, patches, cotangent, pos_kept, pos_sent, bias, table_shard), refs = refs[:7], refs[7:]
+    attn_shards, refs = refs[:layers], refs[layers:]
+    mlp_shards, refs = refs[:layers], refs[layers:]
+    (final, chip_cot, pos_back, narrow, up_bias), refs = refs[:5], refs[5:]
+    mlp_fulls, refs = refs[:layers], refs[layers:]
+    kept, refs = refs[: 12 * layers], refs[12 * layers :]
+    (
+        table_full, attn_full, table, weights, mlp_block, sorted_rows, arrived_rows, middle, act, query,
+        key, value, key_sib, value_sib, exact, mixed, lse, hidden, slope, keys, values,
+        send, recv, local, swap_send, swap_recv, save_sem, load_sem,
+    ) = refs
+    state = final
+    place = my_place()
+    z, x, y, core = place
+    rows, features = state.shape
+    slots = rows // 2
+    halves = [slice(0, slots), slice(slots, rows)]
+    blocks = mlp_fulls[0].shape[0] * mlp_fulls[0].shape[1]
+    to_y, to_core = device_at(z, x, 1 - y, core), device_at(z, x, y, 1 - core)
+    score_scale = HEAD_DIM ** (-0.5) * LOG2_E
+
+    def gather(slot, shard, full, order, start, size):
+        return Gather(
+            place, shard, full, order, start, size, send.at[slot], recv.at[slot], local.at[slot]
+        )
+
+    gathers = [gather(0, table_shard, table_full, "zxy", 0, table_shard.shape[0])]
+    for layer in range(layers):
+        slot = 1 + 3 * layer
+        gathers.append(gather(slot, attn_shards[layer], attn_full.at[layer], "zxy", 0, 4 * owned))
+        for part in range(2):
+            gathers.append(
+                gather(
+                    slot + 1 + part, mlp_shards[layer], mlp_fulls[layer], "yzx", part * up_rows, up_rows
+                )
+            )
+    chain = GatherChain(gathers)
+
+    def swap(slot, src, dst, device):
+        return remote(src, dst, swap_send.at[slot], swap_recv.at[slot], device)
+
+    greet_signal(place)
+    greet_wait()
+    chain.begin()
+    send_pos = swap(0, pos_sent, pos_back, to_y)
+    send_pos.start()
+    sorted_rows[...] = dot_nn(choose[...], patches[...]).astype(BF16)
+    send_rows = swap(1, sorted_rows.at[halves[1]], arrived_rows, to_y)
+    send_rows.start()
+    chain.follow()
+    chip_cot[halves[0]] = dot_nn(choose[halves[0]], cotangent[...]).astype(BF16)
+    chain.turn(0)
+    send_pos.wait()
+    send_rows.wait()
+    chain.finish(0)
+
+    devices = 32
+    for a in range(4):
+        block = table_full[a].reshape(8, owned + 8, table.shape[1]).astype(F32)
+        table[a * 8 * owned : (a + 1) * 8 * owned] = (
+            block[:, :owned].reshape(8 * owned, table.shape[1]).astype(BF16)
+        )
+    lane = lax.broadcasted_iota(jnp.int32, (devices, 1, features), 2)
+    device = lax.broadcasted_iota(jnp.int32, (devices, 1, features), 0)
+    for b in range(3):
+        width = owned if b < 2 else 4 * owned
+        packed = table_full[:, :, :, :, owned:, b * LANES : (b + 1) * LANES]
+        packed = packed.reshape(devices * 8, LANES)
+        wide = dot_nn(packed, spread_matrix(width, features)).reshape(devices, 8, features)
+        if b < 2:
+            wide = jnp.where(lane // owned == device, wide, 0.0)
+            narrow[8 * b : 8 * b + 8] = jnp.sum(wide, axis=0)
+        else:
+            wide = jnp.where(lane // width == lax.rem(device, 8), wide, 0.0)
+            up_bias[...] = jnp.sum(wide.reshape(4, 8, 8, features), axis=1)
+
+    position = lax.broadcasted_iota(jnp.int32, (slots, table.shape[1]), 1).astype(F32)
+    for at, pos, row_ref in ((halves[0], pos_kept, sorted_rows), (halves[1], pos_back, arrived_rows)):
+        column = jnp.transpose(jnp.broadcast_to(pos[0:1, 0:slots], (LANES, slots)))[:, 0:1]
+        lookup = (position == column).astype(F32).astype(BF16)
+        state[at] = row_ref[0:slots].astype(F32) + dot_nt(lookup, table[...])
+
+    def save(layer, index, ref):
+        return local_copy(ref, kept[12 * layer + index], save_sem.at[index])
+
+    def save_block(layer, index, block):
+        ref = (hidden, slope)[index - 10].at[lax.rem(block, 2)]
+        return local_copy(ref, kept[12 * layer + index].at[block], save_sem.at[index + 2 * lax.rem(block, 2)])
+
+    def load_block(layer, block):
+        slot = lax.rem(block, 2)
+        return local_copy(
+            mlp_fulls[layer].at[block // 2, lax.rem(block, 2)], mlp_block.at[slot], load_sem.at[slot]
+        )
+
+    def attend_pair(pair, layer):
+        at_lanes = pl.ds(pl.multiple_of(pair * LANES, LANES), LANES)
+        values[halves[0]] = value[halves[0], at_lanes]
+        values[halves[1]] = value[halves[1], at_lanes]
+        values[rows : rows + slots] = value_sib[layer, halves[0], at_lanes]
+        values[rows + slots :] = value_sib[layer, halves[1], at_lanes]
+        lanes = lax.broadcasted_iota(jnp.int32, (1, LANES), 1)
+        results = [[], []]
+        totals = [[], []]
+        for head in range(2):
+            lane, own, spare = lane_marks(head)
+            own16 = own.astype(BF16)
+            at_spare = (lane == spare).astype(BF16)
+            keys[0:rows] = key[:, at_lanes] * own16 + bias[0:rows] * at_spare
+            keys[rows:] = key_sib[layer, :, at_lanes] * own16 + bias[rows:] * at_spare
+            for at in halves:
+                scores = dot_nt(query[at, at_lanes] * own16 + at_spare, keys[...])
+                top = jnp.max(scores, axis=-1, keepdims=True)
+                weight = jnp.exp2(scores - top)
+                total = jnp.sum(weight, axis=-1, keepdims=True)
+                results[head].append(dot_nn(weight.astype(BF16), values[...]) * (1.0 / total))
+                totals[head].append(top + jnp.log2(total))
+        for index, at in enumerate(halves):
+            both = jnp.where(lanes < HEAD_DIM, results[0][index], results[1][index])
+            mixed[at, at_lanes] = both.astype(BF16)
+            exact[at, at_lanes] = both
+            held = lse[at]
+            held = jnp.where(lanes == 2 * pair, totals[0][index], held)
+            lse[at] = jnp.where(lanes == 2 * pair + 1, totals[1][index], held)
+
+    def saved_refs(layer):
+        return (query, key, value, key_sib.at[layer], value_sib.at[layer], exact)
+
+    lse[...] = jnp.zeros_like(lse)
+    for layer in range(layers):
+        after = layer > 0
+        base = count * layer
+
+        def line(index):
+            return narrow[base + index : base + index + 1]
+
+        save(layer, 0, state).start()
+        for at in halves:
+            normed, unused = norm_parts(state[at])
+            act[at] = (normed * line(0) + line(1)).astype(BF16)
+        if not after:
+            chain.turn(1)
+        chain.finish(1 + 3 * layer)
+        if after:
+            save(layer - 1, 1, weights).wait()
+        for a in range(4):
+            block = attn_full[layer, a].reshape(8, 4 * owned, features).astype(F32)
+            for index in range(4):
+                part = block[:, index * owned : (index + 1) * owned].reshape(8 * owned, features)
+                weights[index, a * 8 * owned : (a + 1) * 8 * owned] = part.astype(BF16)
+        save(layer, 1, weights).start()
+        if after:
+            for index in range(2, 8):
+                save(layer - 1, index, saved_refs(layer - 1)[index - 2]).wait()
+            save(layer - 1, 8, lse).wait()
+        for at in halves:
+            key[at] = dot_nn(act[at], weights[1]).astype(BF16)
+        swap(2 + 2 * layer, key, key_sib.at[layer], to_core).start()
+        for at in halves:
+            value[at] = (dot_nn(act[at], weights[2]) + line(3)).astype(BF16)
+        swap(3 + 2 * layer, value, value_sib.at[layer], to_core).start()
+        for at in halves:
+            query[at] = ((dot_nn(act[at], weights[0]) + line(2)) * score_scale).astype(BF16)
+        swap(2 + 2 * layer, key, key_sib.at[layer], to_core).wait()
+        swap(3 + 2 * layer, value, value_sib.at[layer], to_core).wait()
+
+        def one_pair(pair, carry, layer=layer):
+            attend_pair(pair, layer)
+            when = 2 if layer == 0 else 0
+            pl.when(pair == when)(lambda: chain.turn(2 + 3 * layer))
+            return carry
+
+        lax.fori_loop(0, features // LANES, one_pair, 0)
+        for index in range(2, 8):
+            save(layer, index, saved_refs(layer)[index - 2]).start()
+        save(layer, 8, lse).start()
+        if after:
+            save(layer - 1, 9, middle).wait()
+        for at in halves:
+            total = state[at] + dot_nn(mixed[at], weights[3]) + line(4)
+            middle[at] = total
+            normed, unused = norm_parts(total)
+            act[at] = (normed * line(5) + line(6)).astype(BF16)
+        save(layer, 9, middle).start()
+        save(layer, 0, state).wait()
+        for at in halves:
+            state[at] = middle[at] + line(7)
+        chain.turn(3 + 3 * layer)
+        chain.finish(2 + 3 * layer)
+        chain.finish(3 + 3 * layer)
+        load_block(layer, 0).start()
+        if layer == layers - 1:
+            sorted_back = swap(2 + 2 * layers, sorted_rows.at[halves[1]], chip_cot.at[halves[1]], to_y)
+            sorted_rows[halves[1]] = dot_nn(choose[halves[1]], cotangent[...]).astype(BF16)
+            sorted_back.start()
+
+        def one_block(block, carry, layer=layer):
+            slot = lax.rem(block, 2)
+            pl.when(block + 1 < blocks)(lambda: load_block(layer, block + 1).start())
+            load_block(layer, block).wait()
+
+            @pl.when(block >= 2)
+            def _():
+                save_block(layer, 10, block - 2).wait()
+                save_block(layer, 11, block - 2).wait()
+
+            weight_up = mlp_block[slot, :, :, 0:up_rows, :].reshape(features, features)
+            weight_down = mlp_block[slot, :, :, up_rows:, :].reshape(features, features)
+            shift = up_bias[block, layer : layer + 1]
+            for at in halves:
+                pre_act = dot_nn(act[at], weight_up) + shift
+                below = 0.5 * (1.0 + lax.erf(pre_act * SQRT_HALF))
+                hidden_part = (pre_act * below).astype(BF16)
+                hidden[slot, at] = hidden_part
+                bend = below + pre_act * jnp.exp(-0.5 * pre_act * pre_act) * NORMAL_PEAK
+                slope[slot, at] = bend.astype(BF16)
+                state[at] += dot_nt(hidden_part, weight_down)
+            save_block(layer, 10, block).start()
+            save_block(layer, 11, block).start()
+            return carry
+
+        lax.fori_loop(0, blocks, one_block, 0)
+        for block in (blocks - 2, blocks - 1):
+            save_block(layer, 10, block).wait()
+            save_block(layer, 11, block).wait()
+        if layer < layers - 1:
+            chain.turn(4 + 3 * layer)
+    last = layers - 1
+    swap(2 + 2 * layers, sorted_rows.at[halves[1]], chip_cot.at[halves[1]], to_y).wait()
+    save(last, 1, weights).wait()
+    for index in range(2, 8):
+        save(last, index, saved_refs(last)[index - 2]).wait()
+    save(last, 8, lse).wait()
+    save(last, 9, middle).wait()
+    chain.drain()
+
+
+def forward(choose, patches, cotangent, pos_kept, pos_sent, bias, table_shard, attn_shards, mlp_shards, count, owned, collective_id):
+    layers = len(attn_shards)
+    rows, features = choose.shape[0], patches.shape[1]
+    deep = mlp_shards[0].shape[0]
+    blocks = 4
+    wide = (rows, features)
+
+    def like(shape, dtype):
+        return jax.ShapeDtypeStruct(shape, dtype)
+
+    saved = [
+        like(wide, F32), like((4, features, features), BF16), *[like(wide, BF16)] * 5, like(wide, F32),
+        like((rows, LANES), F32), like(wide, F32), *[like((blocks,) + wide, BF16)] * 2,
+    ]
+    out_shape = [
+        like(wide, F32), like(wide, BF16), like(pos_sent.shape, F32), like((layers * count, features), F32),
+        like((blocks, 8, features), F32),
+        *[like((2, 2, 4, 2, deep, features), BF16)] * layers,
+        *(saved * layers),
+    ]
+    groups = 1 + 3 * layers
+    half16 = pltpu.VMEM((rows // 2, features), BF16)
+    wide16, wide32 = pltpu.VMEM(wide, BF16), pltpu.VMEM(wide, F32)
+    each16 = pltpu.VMEM((layers,) + wide, BF16)
+    scratch = [
+        pltpu.VMEM((4, 2, 2, 2) + table_shard.shape, BF16),
+        pltpu.VMEM((layers, 4, 2, 2, 2, 4 * owned, features), BF16),
+        pltpu.VMEM((features, table_shard.shape[1]), BF16),
+        pltpu.VMEM((4, features, features), BF16),
+        pltpu.VMEM((2, 4, 2, deep, features), BF16),
+        wide16, half16, wide32, wide16, wide16, wide16, wide16, each16, each16, wide32, wide16,
+        pltpu.VMEM((rows, LANES), F32),
+        pltpu.VMEM((2,) + wide, BF16),
+        pltpu.VMEM((2,) + wide, BF16),
+        pltpu.VMEM((2 * rows, LANES), BF16),
+        pltpu.VMEM((2 * rows, LANES), BF16),
+        pltpu.SemaphoreType.DMA((groups, 8)),
+        pltpu.SemaphoreType.DMA((groups, 8)),
+        dma_sems(groups),
+        dma_sems(3 + 2 * layers),
+        dma_sems(3 + 2 * layers),
+        dma_sems(14),
+        dma_sems(2),
+    ]
+    args = (choose, patches, cotangent, pos_kept, pos_sent, bias, table_shard, *attn_shards, *mlp_shards)
+    results = pl.pallas_call(
+        functools.partial(forward_kernel, (layers, count, owned, deep // 2)),
+        out_shape=out_shape,
+        in_specs=[vmem()] * len(args),
+        out_specs=[vmem()] * 5 + [hbm()] * (len(out_shape) - 5),
+        scratch_shapes=scratch,
+        compiler_params=pltpu.CompilerParams(
+            collective_id=collective_id, has_side_effects=True, vmem_limit_bytes=VMEM_LIMIT
+        ),
+        name="forward",
+    )(*args)
+    mlp_fulls = results[5 : 5 + layers]
+    kept = results[5 + layers :]
+    return results[:5], mlp_fulls, [kept[12 * i : 12 * i + 12] for i in range(layers)]
+
+
+def split_rows(values):
+    high = values.astype(BF16)
+    rest = values - high.astype(F32)
+    middle = rest.astype(BF16)
+    return high, middle, (rest - middle.astype(F32)).astype(BF16)
+
+
+def chip_shards(
+    patches,
+    clip_of_row,
+    position_of_row,
+    pos_embed,
+    norm1_gain,
+    norm1_bias,
+    query_bias,
+    value_bias,
+    out_bias,
+    norm2_gain,
+    norm2_bias,
+    up_bias,
+    down_bias,
+    qkv_weight,
+    out_weight,
+    up_weight,
+    down_weight,
+    cotangent,
+):
+    layers, owned, features = qkv_weight.shape[0], qkv_weight.shape[1], patches.shape[1]
+    pieces = lax.axis_size("gy")
+    piece_rows = patches.shape[0]
+    devices = features // owned
+    positions = pos_embed.shape[0]
+    padded_positions = -(-positions // 256) * 256
+    slots = -(-positions // pieces)
+    slots = -(-slots // 16) * 16
+    rows = 2 * slots
+    hidden_width = up_weight.shape[2]
+    up_rows = up_weight.shape[1]
+    gy = lax.axis_index("gy")
+    side, core = gy // 2, lax.rem(gy, 2)
+
+    low_clip, high_clip = jnp.min(clip_of_row), jnp.max(clip_of_row)
+    low_is_long = 2 * jnp.sum((clip_of_row == low_clip).astype(jnp.int32)) > clip_of_row.shape[0]
+    long_clip = jnp.where(low_is_long, low_clip, high_clip)
+    kept_all = ((clip_of_row == long_clip) == (side == 0)).reshape(pieces, piece_rows)
+    kept_count = jnp.sum(kept_all.astype(jnp.int32), axis=1)
+    kept = lax.dynamic_index_in_dim(kept_all, gy, 0, keepdims=False)
+    rank_kept = jnp.cumsum(kept.astype(jnp.int32)) - 1
+    rank_sent = jnp.arange(piece_rows, dtype=jnp.int32) - rank_kept - 1
+    slot = jnp.arange(slots, dtype=jnp.int32)[:, None]
+    pick_kept = (slot == rank_kept[None]) & kept[None]
+    pick_sent = (slot == rank_sent[None]) & jnp.logical_not(kept)[None]
+    choose = jnp.concatenate([pick_kept, pick_sent], axis=0)
+    choose16 = choose.astype(BF16)
+    sorted_positions = jnp.sum(jnp.where(choose, position_of_row[None], 0), axis=1).astype(F32)
+    pos_kept, pos_sent = (
+        jnp.broadcast_to(jnp.pad(part, (0, -slots % LANES))[None], (8, slots + -slots % LANES))
+        for part in (sorted_positions[:slots], sorted_positions[slots:])
+    )
+
+    def slot_bias(of_core):
+        mine = lax.dynamic_index_in_dim(kept_count, side * 2 + of_core, 0, keepdims=False)
+        theirs = lax.dynamic_index_in_dim(kept_count, (1 - side) * 2 + of_core, 0, keepdims=False)
+        steps = jnp.arange(slots, dtype=jnp.int32)
+        used = jnp.concatenate([steps < mine, steps < theirs])
+        return jnp.where(used, 0.0, MASKED)
+
+    bias = jnp.concatenate([slot_bias(core), slot_bias(1 - core)]).astype(BF16)
+    bias = jnp.broadcast_to(bias[:, None], (2 * rows, LANES))
+
+    narrow = jnp.stack(
+        [norm1_gain, norm1_bias, query_bias, value_bias, out_bias, norm2_gain, norm2_bias, down_bias],
+        axis=1,
+    )
+    count = narrow.shape[1]
+    small = jnp.concatenate(
+        [
+            jnp.pad(narrow.reshape(layers * count, owned), ((0, 0), (0, LANES - owned))),
+            jnp.pad(up_bias, ((0, 8 - layers), (0, LANES - up_bias.shape[1]))),
+        ],
+        axis=0,
+    )
+    small = jnp.transpose(small.reshape(layers + 1, 8, LANES), (1, 0, 2)).reshape(8, -1)
+    table_shard = jnp.concatenate(
+        [
+            jnp.pad(pos_embed.T, ((0, 0), (0, padded_positions - positions))),
+            jnp.pad(small, ((0, 0), (0, padded_positions - small.shape[1]))),
+        ],
+        axis=0,
+    )
+    attn_shards, mlp_shards = [], []
+    for layer in range(layers):
+        qkv = jnp.transpose(qkv_weight[layer].reshape(owned, 3, features), (1, 0, 2))
+        attn_shards.append(jnp.concatenate([qkv.reshape(3 * owned, features), out_weight[layer]], axis=0))
+        mlp_shards.append(jnp.concatenate([up_weight[layer], down_weight[layer].T], axis=0))
+    (state, chip_cotangent, pos_back, narrow_all, unused_up), mlp_fulls, stored = forward(
+        choose16, patches, cotangent, pos_kept, pos_sent, bias, table_shard, attn_shards, mlp_shards,
+        count, owned, 0,
+    )
+    row_positions = jnp.concatenate([pos_kept[0, :slots], pos_back[0, :slots]])
+    position_ids = jnp.arange(padded_positions, dtype=jnp.int32).astype(F32)
+    lookup = (row_positions[:, None] == position_ids[None]).astype(BF16)
+    split = layers * count * owned
+
+    def from_chip(values_own, values_back):
+        both = jnp.concatenate([values_own, values_back], axis=0)
+        parts = split_rows(both)
+        return sum(dot_tn(choose16, part) for part in parts)
+
+    activations = from_chip(state[:slots], to_partner(state[slots:]))
+
+    def by_owner(part):
+        return part.reshape(devices, owned, part.shape[1])
+
+    gradient = chip_cotangent.astype(F32)
+    narrow_parts, up_bias_parts = ([None] * layers for _ in range(2))
+    mlp_sums, attn_sums = ([None] * layers for _ in range(2))
+    mlp_done = attn_part = None
+    for layer in reversed(range(layers)):
+        (before, weights, queries, key_rows, value_rows, key_sib, value_sib, exact, lse, middle,
+         hidden, slope) = stored[layer]
+        weight_q, weight_k, weight_v, weight_o = (weights[i] for i in range(4))
+        mlp_full = mlp_fulls[layer]
+        gain_one, shift_one, gain_two, shift_two = (narrow_all[count * layer + i] for i in (0, 1, 5, 6))
+        act_one = (norm_parts(before)[0] * gain_one + shift_one).astype(BF16)
+        mixed = exact.astype(BF16)
+        ids = 8 + 3 * layer
+        entries = []
+        if layer < layers - 1:
+            core_sum = jax.ShapeDtypeStruct(*SumCore(attn_part).outs[0])
+            entries = [
+                (SumCore(attn_part), attn_part, (1, 2)),
+                (SumXY(core_sum, "zxy"), 0, (2, 3, 4)),
+                (SumZ(mlp_done), mlp_done, (1, 4)),
+            ]
+        (mid_grad, lines, up_lines, mlp_part), carried = feed_forward_backward(
+            gradient, middle, gain_two[None], shift_two[None], hidden, slope, mlp_full,
+            Carried(*entries), ids,
+        )
+        gain_two_part, shift_two_part, down_bias_part = lines[0], lines[1], lines[2]
+        up_bias_parts[layer] = up_lines.reshape(-1)
+        entries = [(SumXY(mlp_part, "yzx"), mlp_part, (0, 4, 6))]
+        if layer < layers - 1:
+            mlp_sums[layer + 1] = carried[2]
+            entries.append((SumZ(carried[1]), carried[1], (0, 6)))
+        grad_one = mid_grad.astype(BF16)
+        out_bias_part = jnp.sum(grad_one.astype(F32), axis=0)
+        out_part = dot_tn(mixed, grad_one)
+        mixed_grad = dot_nt(grad_one, weight_o).astype(BF16)
+        (query_grad, key_own, key_far, value_own, value_far), carried = attention_backward(
+            queries, key_rows, key_sib, value_rows, value_sib, mixed_grad, exact, lse, bias,
+            Carried(*entries), ids + 1,
+        )
+        mlp_done = carried[0]
+        if layer < layers - 1:
+            attn_sums[layer + 1] = carried[1]
+        key_grad = (key_own.astype(F32) + to_sibling(key_far).astype(F32)).astype(BF16)
+        value_grad = (value_own.astype(F32) + to_sibling(value_far).astype(F32)).astype(BF16)
+        query_bias_part = jnp.sum(query_grad.astype(F32), axis=0)
+        value_bias_part = jnp.sum(value_grad.astype(F32), axis=0)
+        attn_part = jnp.concatenate(
+            [by_owner(dot_tn(act_one, g)) for g in (query_grad, key_grad, value_grad)]
+            + [by_owner(out_part)],
+            axis=1,
+        ).astype(BF16).reshape(4, 2, 2, 2, 4 * owned, features)
+        act_one_grad = (
+            dot_nt(query_grad, weight_q) + dot_nt(key_grad, weight_k) + dot_nt(value_grad, weight_v)
+        )
+        back_one, gain_one_part, shift_one_part = norm_back(before, gain_one, act_one_grad)
+        gradient = mid_grad + back_one
+        narrow_parts[layer] = jnp.stack(
+            [gain_one_part[0], shift_one_part[0], query_bias_part, value_bias_part, out_bias_part,
+             gain_two_part, shift_two_part, down_bias_part]
+        )
+    input_grad = from_chip(gradient[:slots], to_partner(gradient[slots:]))
+
+    table_part = dot_tn(gradient.astype(BF16), lookup)
+    narrow_part = jnp.transpose(
+        jnp.stack(narrow_parts).reshape(layers, count, devices, owned), (2, 0, 1, 3)
+    ).reshape(devices, split)
+    up_bias_part = jnp.transpose(
+        jnp.stack(up_bias_parts).reshape(layers, devices, -1), (1, 0, 2)
+    ).reshape(devices, -1)
+    small_part = jnp.concatenate([narrow_part, up_bias_part], axis=1)[:, None]
+    table_parts = jnp.concatenate(
+        [
+            by_owner(table_part),
+            jnp.pad(small_part, ((0, 0), (0, 7), (0, padded_positions - small_part.shape[2]))),
+        ],
+        axis=1,
+    ).astype(BF16)
+    table_parts = table_parts.reshape((4, 2, 2, 2) + table_parts.shape[1:])
+    cores = [SumCore(attn_part), SumCore(table_parts)]
+    core_sums = [jax.ShapeDtypeStruct(*stage.outs[0]) for stage in cores]
+    crosses = [SumXY(core_sums[0], "zxy"), SumXY(core_sums[1], "zxy")]
+    cross_sums = [jax.ShapeDtypeStruct(*stage.outs[0]) for stage in crosses]
+    ends = [SumZ(mlp_done), SumZ(cross_sums[0]), SumZ(cross_sums[1])]
+    sums = run_stages(
+        [*cores, *crosses, *ends],
+        [attn_part, table_parts, 0, 1, mlp_done, 2, 3],
+        [(0, 0), (1, 0), (4, 0), (0, 1), (2, 0), (1, 1), (3, 0), (2, 1), (3, 1), (2, 2), (5, 0), (3, 2)]
+        + [(6, 0), (4, 1), (5, 1), (6, 1)],
+        14,
+        "sum_last",
+    )
+    mlp_sums[0], attn_sums[0], table_sum = sums[4], sums[5], sums[6]
+    pos_embed_grad = table_sum[:owned, :positions].T
+    small_sum = table_sum[owned, : small_part.shape[2]]
+    narrow_sum = small_sum[:split].reshape(layers, count, owned)
+    up_bias_grad = small_sum[split:].reshape(layers, -1)
+    qkv_weight_grad = jnp.stack(
+        [
+            jnp.transpose(part[: 3 * owned].reshape(3, owned, features), (1, 0, 2)).reshape(owned, -1)
+            for part in attn_sums
+        ]
+    )
+    out_weight_grad = jnp.stack([part[3 * owned :] for part in attn_sums])
+    up_weight_grad = jnp.stack([part[:up_rows] for part in mlp_sums])
+    down_weight_grad = jnp.stack([part[up_rows:].T for part in mlp_sums])
+    return (
+        activations,
+        input_grad,
+        pos_embed_grad,
+        *(narrow_sum[:, i] for i in range(7)),
+        up_bias_grad,
+        narrow_sum[:, 7],
+        qkv_weight_grad,
+        out_weight_grad,
+        up_weight_grad,
+        down_weight_grad,
+    )
+
+
 def solution(mesh):
     return jax.shard_map(
-        shards,
+        chip_shards if mesh.shape["gx"] == 8 and mesh.shape["gy"] == 4 else shards,
         mesh=mesh,
         in_specs=(
             P(("gx", "gy"), None),

time: 1900 us -> 581 us (0.31)
  waiting for transfers between devices: 950 us -> 12.6 us
  Pallas kernels: 0 us -> 422 us
  blocking collectives: 384 us -> 0 us
  matrix products: 237 us -> 58.9 us
  local copies, waits for them, and re-layouts: 186 us -> 33.2 us
  other arithmetic: 95.4 us -> 36.5 us
    pallas_call x0 -> x6, Pallas kernels: none -> 422 us  [the longest x4 184 us: carrying(): pl.pallas_call(kernel, grid=(steps,), out_shape=[*out_shape, *carried.out...]
    reduce_scatter x7 -> x0, waiting for transfers between devices: 402 us -> none  [the longest x1 168 us: shards(): lax.psum_scatter(stacked_member(collected, 9), ('gx', 'gy'), scatter_dime...]
    unnamed x34 -> x0, waiting for transfers between devices: 373 us -> none
    all_gather x9 -> x0, blocking collectives: 343 us -> none  [the longest x1 43.2 us: shards(): lax.all_gather(norm1_gain, ('gx', 'gy'), axis=1, tiled=True)]
    dot_general x108 -> x23, matrix products: 237 us -> 58.9 us  [the longest x15 32.7 us: dot_tn(): lax.dot_general(left, right, (((0,), (0,)), ((), ())), preferred_element_...]
    all_gather x13 -> x0, waiting for transfers between devices: 176 us -> none  [the longest x1 49.2 us: shards(): lax.all_gather(qkv_weight, ('gx', 'gy'), axis=1, tiled=True)]
    dynamic_slice x109 -> x1, local copies, waits for them, and re-layouts: 72.3 us -> 0.61 us  [slot_bias(): lax.dynamic_index_in_dim(kept_count, side * 2 + of_core, 0, keepdims=False)]
    unnamed x220 -> x102, local copies, waits for them, and re-layouts: 76.2 us -> 9.89 us
  transfers between devices with their start and end apart: 27 -> 6, of which waited for: 19 -> 1; matrix products, arithmetic and copies ran while one was open for 12% -> 12% of each run, Pallas kernels for 0% -> 32%
where the time goes in v2:
time: 581 us; the launch traced here: 570 us
  Pallas kernels  422 us (73%)
  matrix products  58.9 us (10%)
  other arithmetic  36.5 us (6%)
  local copies, waits for them, and re-layouts  33.2 us (6%)
  waiting for transfers between devices  12.6 us (2%)
    pallas_call x4, Pallas kernels, carrying(): pl.pallas_call(kernel, grid=(steps,), out_shape=[*out_shape, *carried.out...  184 us
    pallas_call x1, Pallas kernels, forward(): pl.pallas_call(functools.partial(forward_kernel, (layers, count, owned, d...  175 us
    pallas_call x1, Pallas kernels, run_stages(): pl.pallas_call(functools.partial(comm_kernel, steps, stages, marks), out_...  62.8 us
    dot_general x15, matrix products, dot_tn(): lax.dot_general(left, right, (((0,), (0,)), ((), ())), preferred_element_...  32.7 us
    dot_general x8, matrix products, dot_nt(): lax.dot_general(left, right, (((1,), (1,)), ((), ())), preferred_element_...  26.2 us
    ppermute x2, waiting for transfers between devices, to_partner(): return lax.ppermute(value, ('gx', 'gy'), flip_pairs(1, 0))  12.6 us
  transfers between devices with their start and end apart: 6, of which 1 were waited for; matrix products, arithmetic and copies ran while one was open for 12% of the time, Pallas kernels for 32%

profile of v2, /device:TPU:0, one launch (start us, length us, event | category | flops | bytes accessed | tf_op | source)
XLA Modules:
  0.0 570.1 jit_solution(2760919226539783303)
XLA Ops:
  0.7 1.4 reduce_min.9
  2.1 2.0 fusion.64
  7.9 0.9 fusion.63.refs_0_
  17.5 1.3 iota_compare_fusion.6
  18.9 1.3 iota_compare_fusion.8
  23.8 0.9 broadcast_in_dim.37.refs_5_.refs_8_
  24.7 175.1 %forward.1 = (f32[608,768]{1,0:T(8,128)}, bf16[608,768]{1,0:T(8,128)(2,1)}, f32[8,384]{1,0:T(8,128)}, f32[16,768]{1,0:T(8,128)}, f32[4,8,768]{2,1,0:T(8,128)}, /...) custom-call(bf16[608,432]{1,0:T(8,128)(2,1)} %fusion.63.refs_0_, ...), custom_call_target="tpu_custom_call" | custom-call | tf_op jit(solution)/shard_map/forward/pallas_call | solution.py:1649
  199.8 2.9 fusion.66
  202.7 1.4 convert_element_type.168.refs_0_
  204.7 37.8 %feed_forward_backward.2 = (f32[608,768]{1,0:T(8,128)}, f32[8,768]{1,0:T(8,128)}, f32[4,1,768]{2,1,0:T(1,128)}, bf16[2,4,2,192,768]{4,3,2,1,0:T(8,128)(2,1)}) custom-call(f32[608,768]{1,0:T(8,128)} %convert_element_type.168.refs_0_, f32[608,768]{1,0:T(8,128)} %get-tuple-element.74.refs_1_, f32[1,768]{1,0:T(1,128)} %get-tuple-element.169.refs_2_, ...), custom_call_target="tpu_custom_call" | custom-call | flops 11475615744 | bytes 38252052 | tf_op jit(solution)/shard_map/feed_forward_backward/pallas_call | solution.py:875
  242.4 3.7 convolution_convert_fusion.10.refs_5_
  246.1 53.2 %attention_backward.2 = (bf16[608,768]{1,0:T(8,128)(2,1)}, bf16[608,768]{1,0:T(8,128)(2,1)}, bf16[608,768]{1,0:T(8,128)(2,1)}, bf16[608,768]{1,0:T(8,128)(2,1)},...) custom-call(bf16[608,768]{1,0:T(8,128)(2,1)} %get-tuple-element.80.refs_0_, ...), custom_call_target="tpu_custom_call" | custom-call | flops 11356078080 | bytes 37853592 | tf_op jit(solution)/shard_map/attention_backward/pallas_call | solution.py:875
  299.9 1.7 convert_reduce_fusion.5
  302.7 3.6 fusion.16
  310.5 3.3 convolution_convert_fusion.5
  313.8 2.6 fusion.14
  316.8 3.1 multiply_reduce_fusion
  319.9 1.1 convolution_convert_fusion.8
  321.4 1.9 multiply_add_fusion.1.refs_0_
  323.3 2.3 convolution_convert_fusion.6
  325.6 2.3 convolution_convert_fusion.7
  327.9 2.4 pad_maximum_fusion.refs_7_
  330.4 46.2 %feed_forward_backward.3 = (f32[608,768]{1,0:T(8,128)}, f32[8,768]{1,0:T(8,128)}, f32[4,1,768]{2,1,0:T(1,128)}, bf16[2,4,2,192,768]{4,3,2,1,0:T(8,128)(2,1)}, bf...) custom-call(f32[608,768]{1,0:T(8,128)} %multiply_add_fusion.1.refs_0_, ...), custom_call_target="tpu_custom_call" | custom-call | flops 11475615744 | bytes 38252052 | tf_op jit(solution)/shard_map/feed_forward_backward/pallas_call | solution.py:875
  376.6 3.7 convolution_convert_fusion.9.refs_5_
  380.3 47.3 %attention_backward.3 = (bf16[608,768]{1,0:T(8,128)(2,1)}, bf16[608,768]{1,0:T(8,128)(2,1)}, bf16[608,768]{1,0:T(8,128)(2,1)}, bf16[608,768]{1,0:T(8,128)(2,1)},...) custom-call(bf16[608,768]{1,0:T(8,128)(2,1)} %get-tuple-element.101.refs_0_, ...), custom_call_target="tpu_custom_call" | custom-call | flops 11356078080 | bytes 37853592 | tf_op jit(solution)/shard_map/attention_backward/pallas_call | solution.py:875
  428.5 1.5 fusion.61
  430.1 1.8 convert_reduce_fusion.4
  431.9 3.6 fusion.10
  435.5 2.0 fusion.34
  437.5 2.0 fusion.40
  439.5 3.1 fusion.6
  446.5 3.3 convolution_convert_fusion.1
  449.8 2.7 fusion.8
  452.5 3.2 multiply_reduce_fusion.1
  456.3 1.4 fusion.65
  458.2 2.1 convolution_convert_fusion.4
  461.1 1.8 fusion.62
  467.3 2.8 convolution_convert_fusion
  470.1 1.9 pad_maximum_fusion.2.refs_1_
  472.0 2.4 convolution_convert_fusion.2
  474.4 2.4 convolution_convert_fusion.3
  476.9 2.4 pad_maximum_fusion.1.refs_0_
  479.3 62.8 %sum_last.1 = (bf16[4,2,2,96,768]{4,3,2,1,0:T(8,128)(2,1)}, bf16[4,2,2,32,1280]{4,3,2,1,0:T(8,128)(2,1)}, bf16[4,96,768]{2,1,0:T(8,128)(2,1)}, bf16[4,32,1280]{2...) custom-call(bf16[4,2,2,2,96,768]{5,4,3,2,1,0:T(8,128)(2,1)} %pad_maximum_fusion.1.refs_0_, ...), custom_call_target="tpu_custom_call" | custom-call | tf_op jit(solution)/shard_map/sum_last/pallas_call | solution.py:827
  543.6 0.9 slice.232
  545.5 1.4 collective-permute-start.5
  548.5 1.1 slice_bitcast_fusion.1
  553.5 12.6 %collective-permute-done.5 = f32[304,768]{1,0:T(8,128)S(1)} collective-permute-done((f32[304,768]{1,0:T(8,128)S(1)}, f32[304,768]{1,0:T(8,128)S(1)}, u32[]{:S(2)}, u32[]{:S(2)}) %collective-permute-start.5) | collective-permute-done | bytes 933920 | tf_op jit(solution)/shard_map/ppermute | solution.py:456
  567.7 1.9 fusion.5
  (216 shorter events, 41.7 us)
Async XLA Ops:
  0.6 15.9 %copy-start.31 = (bf16[2,24,2304]{2,1,0:T(8,128)(2,1)S(1)}, bf16[2,24,2304]{2,1,0:T(8,128)(2,1)}, u32[]{:S(2)}) copy-start(bf16[2,24,2304]{2,1,0:T(8,128)(2,1)} %param.31) | copy-start | bytes 663556
  0.7 16.1 %copy-start.28 = (bf16[2,768,96]{1,2,0:T(8,128)(2,1)S(1)}, bf16[2,768,96]{1,2,0:T(8,128)(2,1)}, u32[]{:S(2)}) copy-start(bf16[2,768,96]{1,2,0:T(8,128)(2,1)} %param.34) | copy-start | bytes 884740
  7.6 9.2 %copy-start.29 = (bf16[2,96,768]{2,1,0:T(8,128)(2,1)S(1)}, bf16[2,96,768]{2,1,0:T(8,128)(2,1)}, u32[]{:S(2)}) copy-start(bf16[2,96,768]{2,1,0:T(8,128)(2,1)} %param.33) | copy-start | bytes 884740
  7.8 12.5 %copy-start.38 = (bf16[2,96]{1,0:T(2,128)(2,1)S(1)}, bf16[2,96]{1,0:T(2,128)(2,1)}, u32[]{:S(2)}) copy-start(bf16[2,96]{1,0:T(2,128)(2,1)} %param.29) | copy-start | bytes 1156
  7.8 12.5 %copy-start.33 = (bf16[1214,24]{0,1:T(8,128)(2,1)S(1)}, bf16[1214,24]{0,1:T(8,128)(2,1)}, u32[]{:S(2)}) copy-start(bf16[1214,24]{0,1:T(8,128)(2,1)} %param.21) | copy-start | bytes 174820
  199.8 2.9 copy-start.24
  202.7 1.4 copy-start.36
  202.7 232.8 %collective-permute-start = (f32[304,768]{1,0:T(8,128)}, f32[304,768]{1,0:T(8,128)}, u32[]{:S(2)}, u32[]{:S(2)}) collective-permute-start(f32[304,768]{1,0:T(8,128)} %get-tuple-element.149), channel_id=1, source_target_pairs={{0,2},{1,3},{2,0},{3,1},{4,6},{5,7},{6,4},{7,5},{8,10},{9,11},{10,... | collective-permute-start | bytes 2801672 | tf_op jit(solution)/shard_map/ppermute | solution.py:456
  299.3 2.3 copy-start.1
  299.3 17.1 %collective-permute-start.2 = (bf16[608,768]{1,0:T(8,128)(2,1)}, bf16[608,768]{1,0:T(8,128)(2,1)}, u32[]{:S(2)}, u32[]{:S(2)}) collective-permute-start(bf16[608,768]{1,0:T(8,128)(2,1)} %get-tuple-element.93), channel_id=1, source_target_pairs={{0,1},{1,0},{2,3},{3,2},{4,5},{5,4},{6,7},{7,6},{8,9},{9,8},{10,11... | collective-permute-start | bytes 2801672 | tf_op jit(solution)/shard_map/ppermute | solution.py:460
  299.5 14.3 %collective-permute-start.1 = (bf16[608,768]{1,0:T(8,128)(2,1)}, bf16[608,768]{1,0:T(8,128)(2,1)}, u32[]{:S(2)}, u32[]{:S(2)}) collective-permute-start(bf16[608,768]{1,0:T(8,128)(2,1)} %get-tuple-element.91), channel_id=1, source_target_pairs={{0,1},{1,0},{2,3},{3,2},{4,5},{5,4},{6,7},{7,6},{8,9},{9,8},{10,11... | collective-permute-start | bytes 2801672 | tf_op jit(solution)/shard_map/ppermute | solution.py:460
  301.6 1.2 copy-start.22
  302.7 3.6 copy-start
  306.4 0.7 copy-start.34
  310.5 3.3 copy-start.41
  313.8 2.7 copy-start.2
  313.8 2.7 copy-start.9
  313.8 3.0 copy-start.13
  316.8 3.1 copy-start.23
  319.9 1.5 copy-start.4
  380.3 47.9 %copy-start.35 = (f32[4,1,768]{2,1,0:T(1,128)S(1)}, f32[4,1,768]{2,1,0:T(1,128)}, u32[]{:S(2)}) copy-start(f32[4,1,768]{2,1,0:T(1,128)} %get-tuple-element.120) | copy-start | bytes 36868
  427.6 24.9 %collective-permute-start.4 = (bf16[608,768]{1,0:T(8,128)(2,1)}, bf16[608,768]{1,0:T(8,128)(2,1)}, u32[]{:S(2)}, u32[]{:S(2)}) collective-permute-start(bf16[608,768]{1,0:T(8,128)(2,1)} %get-tuple-element.115), channel_id=1, source_target_pairs={{0,1},{1,0},{2,3},{3,2},{4,5},{5,4},{6,7},{7,6},{8,9},{9,8},{10,11... | collective-permute-start | bytes 2801672 | tf_op jit(solution)/shard_map/ppermute | solution.py:460
  427.7 22.1 %collective-permute-start.3 = (bf16[608,768]{1,0:T(8,128)(2,1)}, bf16[608,768]{1,0:T(8,128)(2,1)}, u32[]{:S(2)}, u32[]{:S(2)}) collective-permute-start(bf16[608,768]{1,0:T(8,128)(2,1)} %get-tuple-element.113), channel_id=1, source_target_pairs={{0,1},{1,0},{2,3},{3,2},{4,5},{5,4},{6,7},{7,6},{8,9},{9,8},{10,11... | collective-permute-start | bytes 2801672 | tf_op jit(solution)/shard_map/ppermute | solution.py:460
  430.0 1.9 copy-start.20
  431.9 3.6 copy-start.10
  439.5 3.2 copy-start.26
  442.6 2.2 copy-start.27
  446.5 3.3 copy-start.39
  449.8 2.7 copy-start.7
  449.8 2.7 copy-start.12
  452.5 3.2 copy-start.3
  455.7 2.5 copy-start.17
  456.3 1.9 copy-start.5
  456.3 1.9 copy-start.21
  460.3 6.9 %copy-start.6 = (f32[608,768]{1,0:T(8,128)S(1)}, f32[608,768]{1,0:T(8,128)}, u32[]{:S(2)}) copy-start(f32[608,768]{1,0:T(8,128)} %copy-done.5) | copy-start | bytes 5603332
  460.3 6.9 %copy-start.37 = (f32[1280]{0:T(1024)S(1)}, f32[1280]{0:T(1024)}, u32[]{:S(2)}) copy-start(f32[1280]{0:T(1024)} %iota_convert_fusion) | copy-start | bytes 15364
  470.1 1.9 copy-start.8
  470.1 1.9 copy-start.18
  472.0 2.4 copy-start.40
  474.4 2.5 copy-start.14
  479.3 66.2 %copy-start.19 = (f32[304,768]{1,0:T(8,128)S(1)}, f32[304,768]{1,0:T(8,128)}, u32[]{:S(2)}) copy-start(f32[304,768]{1,0:T(8,128)} %get-tuple-element.147) | copy-start | bytes 2801668
  542.1 7.5 %copy-start.30 = (f32[1,24,768]{2,1,0:T(8,128)S(1)}, f32[1,24,768]{2,1,0:T(8,128)}, u32[]{:S(2)}) copy-start(f32[1,24,768]{2,1,0:T(8,128)} %slice_bitcast_fusion.9) | copy-start | bytes 221188
  542.1 8.2 %copy-start.16 = (f32[1,96,768]{2,1,0:T(8,128)S(1)}, f32[1,96,768]{2,1,0:T(8,128)}, u32[]{:S(2)}) copy-start(f32[1,96,768]{2,1,0:T(8,128)} %get-tuple-element.153) | copy-start | bytes 884740
  545.5 5.7 copy-start.15
  545.5 20.6 %collective-permute-start.5 = (f32[304,768]{1,0:T(8,128)S(1)}, f32[304,768]{1,0:T(8,128)S(1)}, u32[]{:S(2)}, u32[]{:S(2)}) collective-permute-start(f32[304,768]{1,0:T(8,128)S(1)} %copy-done.19), channel_id=1, source_target_pairs={{0,2},{1,3},{2,0},{3,1},{4,6},{5,7},{6,4},{7,5},{8,10},{9,11},{10,... | collective-permute-start | bytes 2801672 | tf_op jit(solution)/shard_map/ppermute | solution.py:456
  548.5 3.6 copy-start.25
  549.6 3.2 copy-start.32
  549.6 16.5 %copy-start.11 = (f32[304,768]{1,0:T(8,128)S(1)}, f32[304,768]{1,0:T(8,128)}, u32[]{:S(2)}) copy-start(f32[304,768]{1,0:T(8,128)} %get-tuple-element.146) | copy-start | bytes 2801668
